TPU v7x, 32 devices: a whole 2x2x4 slice. The times are simulated.
32 devices in a mesh: pipe: 4 (over y, x), dp: 2 (over core), expert: 4 (over z).
Axes of the slice: x: 2, y: 2, z: 4, core: 2. Of those that a mesh axis runs over, the one named last changes fastest.
Arguments:
- fwd_tokens: bfloat16 [4, 512, 7168], P('pipe', 'expert'), may hold values from -6 to 6
- fwd_routes: int32 [4, 512, 2], P('pipe', 'expert'), may hold values from 0 to 3, all different within a row; in each aligned block of 128 rows (0 to 127, 128 to 255, ..., all dimensions but the last counted through in order) at most 96 rows name the same one
- fwd_gates: float32 [4, 512, 2], P('pipe', 'expert'), may hold values from 0.2 to 1
- bwd_saved: bfloat16 [4, 512, 7168], P('pipe', 'expert'), may hold values from -6 to 6
- bwd_grads: bfloat16 [4, 512, 7168], P('pipe', 'expert'), may hold values from -6 to 6
- bwd_routes: int32 [4, 512, 2], P('pipe', 'expert'), may hold values from 0 to 3, all different within a row; in each aligned block of 128 rows (0 to 127, 128 to 255, ..., all dimensions but the last counted through in order) at most 96 rows name the same one
- bwd_gates: float32 [4, 512, 2], P('pipe', 'expert'), may hold values from 0.2 to 1
- w_up: bfloat16 [4, 4, 7168, 1024], P('pipe', 'expert', None, 'dp'), may hold values from -0.0625 to 0.0625
- w_down: bfloat16 [4, 4, 1024, 7168], P('pipe', 'expert', 'dp'), may hold values from -0.1875 to 0.1875
- query_latent: bfloat16 [4, 2, 1024, 768], P('pipe', 'dp', 'expert'), may hold values from -6 to 6
- key_latent: bfloat16 [4, 2, 1024, 512], P('pipe', 'dp', 'expert'), may hold values from -6 to 6
- query_weight: bfloat16 [4, 768, 8192], P('pipe', None, 'expert'), may hold values from -500 to 500
- key_weight: bfloat16 [4, 512, 8192], P('pipe', None, 'expert'), may hold values from -0.25 to 0.25
Outputs:
- fwd_arrive: bfloat16 [4, 512, 7168], P('pipe', 'expert')
- bwd_arrive: bfloat16 [4, 512, 7168], P('pipe', 'expert')
- query_clipped: bfloat16 [4, 768, 8192], P('pipe', None, 'expert')
- key_clipped: bfloat16 [4, 512, 8192], P('pipe', None, 'expert')
Inputs may be any that keep to these rules, and one draw needn't show every extreme that they name: `fwd_routes`: within the rows of one device (aligned blocks of 128 token rows of a section) no expert is named by more than 96 rows, a bound that some block reaches. `bwd_routes`: within the rows of one device (aligned blocks of 128 token rows of a section) no expert is named by more than 96 rows, a bound that some block reaches.
All inputs are finite; a program needn't handle non-finite values.
Results may differ from a plain program's by a relative error of at most 0.0046.
Values may be sent and summed in bfloat16 or wider, within the bound.
A program may use at most 192 MiB of HBM per device.

v0:
```python
import jax
import jax.numpy as jnp
from jax import lax
from jax.sharding import PartitionSpec as P

HD = 128


clip_limit = 100.0
logit_scale = 192.0 ** (-0.5)


def shifted(block, axis, distance):
    devices = range(lax.axis_size(axis))
    route = [(i - distance, i) for i in devices if i - distance in devices]
    return lax.ppermute(block, axis, route)


def silu_grad(pre_act):
    sigmoid_val = jax.nn.sigmoid(pre_act)
    return sigmoid_val * (1.0 + pre_act * (1.0 - sigmoid_val))


def forward_rows(arrived, up_half, down_half):
    pre_act = jnp.einsum(
        "scd,dh->sch", arrived[:, :, 0], up_half, preferred_element_type=jnp.float32
    )
    hidden = jax.nn.silu(pre_act).astype(jnp.bfloat16)
    return jnp.einsum("sch,hd->scd", hidden, down_half, preferred_element_type=jnp.float32)


def backward_rows(arrived, up_half, down_half):
    pre_act = jnp.einsum(
        "scd,dh->sch", arrived[:, :, 0], up_half, preferred_element_type=jnp.float32
    )
    back_grad = jnp.einsum(
        "scd,hd->sch", arrived[:, :, 1], down_half, preferred_element_type=jnp.float32
    )
    pre_grad = (back_grad * silu_grad(pre_act)).astype(jnp.bfloat16)
    return jnp.einsum("sch,dh->scd", pre_grad, up_half, preferred_element_type=jnp.float32)


def route_through(stacked, routes, gate_vals, up_half, down_half, expert_fn):
    tok_count, top_count = routes.shape
    model_width = stacked.shape[2]
    dest_count = lax.axis_size("expert")
    capacity = 3 * tok_count * top_count // (2 * dest_count)
    flat_ids = routes.reshape(-1)
    row_count = flat_ids.shape[0]
    onehot = (flat_ids[:, None] == jnp.arange(dest_count, dtype=jnp.int32)[None, :]).astype(
        jnp.int32
    )
    slot_rank = jnp.sum((jnp.cumsum(onehot, axis=0) - 1) * onehot, axis=1)
    slot_table = jnp.full((dest_count, capacity), row_count, jnp.int32)
    slot_table = slot_table.at[flat_ids, slot_rank].set(jnp.arange(row_count, dtype=jnp.int32))
    filled = slot_table < row_count
    source = jnp.minimum(slot_table, row_count - 1) // top_count
    outgoing = jnp.where(filled[:, :, None, None], stacked[source], jnp.zeros((), stacked.dtype))
    pieces = expert_fn(
        lax.all_to_all(outgoing, "expert", split_axis=0, concat_axis=0, tiled=True),
        up_half,
        down_half,
    ).astype(jnp.bfloat16)
    returned = lax.all_to_all(pieces, "expert", split_axis=0, concat_axis=0, tiled=True)
    picked = returned[flat_ids, slot_rank].astype(jnp.float32)
    routed = lax.psum(picked.astype(jnp.bfloat16), "dp")
    routed = routed.astype(jnp.float32).reshape(tok_count, top_count, model_width)
    return jnp.sum(gate_vals[:, :, None] * routed, axis=1)


def on_device(
    fwd_tokens,
    fwd_routes,
    fwd_gates,
    bwd_saved,
    bwd_grads,
    bwd_routes,
    bwd_gates,
    w_up,
    w_down,
    query_latent,
    key_latent,
    query_weight,
    key_weight,
):
    up_half = w_up[0, 0]
    down_half = w_down[0, 0]
    tokens_now = fwd_tokens[0]
    fwd_sum = route_through(
        tokens_now[:, None, :], fwd_routes[0], fwd_gates[0], up_half, down_half, forward_rows
    )
    section_out = (tokens_now.astype(jnp.float32) + fwd_sum).astype(jnp.bfloat16)
    grads_now = bwd_grads[0]
    stacked_back = jnp.stack([bwd_saved[0], grads_now], axis=1)
    bwd_sum = route_through(
        stacked_back, bwd_routes[0], bwd_gates[0], up_half, down_half, backward_rows
    )
    input_grad = (grads_now.astype(jnp.float32) + bwd_sum).astype(jnp.bfloat16)
    query_proj = query_weight[0]
    key_proj = key_weight[0]
    heads_here = query_proj.shape[1] // HD
    queries = jnp.dot(
        lax.all_gather(query_latent[0, 0], "expert", axis=0, tiled=True),
        query_proj,
        preferred_element_type=jnp.float32,
    ).astype(jnp.bfloat16)
    seq_len = queries.shape[0]
    queries = queries.reshape(seq_len, heads_here, HD)
    query_pos = jnp.arange(seq_len, dtype=jnp.int32)
    initial = jnp.full((heads_here,), -1e30, jnp.float32)
    shard_rows = lax.all_gather(key_latent[0, 0], "expert", axis=0, tiled=True)
    key_rows = jnp.dot(shard_rows, key_proj, preferred_element_type=jnp.float32).astype(
        jnp.bfloat16
    )
    key_rows = key_rows.reshape(shard_rows.shape[0], heads_here, HD)
    score_matrix = (
        jnp.einsum("qhd,khd->hqk", queries, key_rows, preferred_element_type=jnp.float32)
        * logit_scale
    )
    key_pos = jnp.arange(shard_rows.shape[0], dtype=jnp.int32)
    allowed = query_pos[:, None] >= key_pos[None, :]
    score_matrix = jnp.where(allowed[None], score_matrix, -1e30)
    local_max = jnp.maximum(initial, jnp.max(score_matrix, axis=(1, 2)))
    head_max = lax.pmax(local_max, "dp")
    factor = jnp.sqrt(clip_limit / jnp.maximum(head_max, clip_limit))
    col_factor = jnp.repeat(factor, HD)
    query_clipped = (query_proj.astype(jnp.float32) * col_factor[None, :]).astype(jnp.bfloat16)
    key_clipped = (key_proj.astype(jnp.float32) * col_factor[None, :]).astype(jnp.bfloat16)
    fwd_arrive = shifted(section_out, "pipe", 1)
    bwd_arrive = shifted(input_grad, "pipe", -1)
    return (fwd_arrive[None], bwd_arrive[None], query_clipped[None], key_clipped[None])


def solution(mesh):
    in_specs = (
        P("pipe", "expert", None),
        P("pipe", "expert", None),
        P("pipe", "expert", None),
        P("pipe", "expert", None),
        P("pipe", "expert", None),
        P("pipe", "expert", None),
        P("pipe", "expert", None),
        P("pipe", "expert", None, "dp"),
        P("pipe", "expert", "dp", None),
        P("pipe", "dp", "expert", None),
        P("pipe", "dp", "expert", None),
        P("pipe", None, "expert"),
        P("pipe", None, "expert"),
    )
    out_specs = (
        P("pipe", "expert", None),
        P("pipe", "expert", None),
        P("pipe", None, "expert"),
        P("pipe", None, "expert"),
    )
    return jax.shard_map(
        on_device, mesh=mesh, in_specs=in_specs, out_specs=out_specs, check_vma=False
    )
```

profile of v0, /device:TPU:19, one launch (start us, length us, event | category | flops | bytes accessed | tf_op | source)
XLA Modules:
  0.0 862.4 jit_solution(7127584341973189760)
XLA Ops:
  11.0 11.4 %scatter_fusion = s32[4,96]{1,0:T(4,128)S(1)} fusion(s32[4,96]{1,0:T(4,128)S(1)} %broadcast.168.clone, s32[256]{0:T(256)S(1)} %bitcast.126, s32[256]{0:T(256)S(1)} %iota.34), kind=kCustom, calls=%fused_computation.4 | custom fusion | bytes 5120 | tf_op jit(solution)/shard_map/scatter | solution.py:55
  42.5 11.4 %scatter_fusion.1 = s32[4,96]{1,0:T(4,128)S(1)} fusion(s32[4,96]{1,0:T(4,128)S(1)} %broadcast.168.clone.1, s32[256]{0:T(256)S(1)} %bitcast.125, s32[256]{0:T(256)S(1)} %iota.35), kind=kCustom, calls=%fused_computation.5 | custom fusion | bytes 5120 | tf_op jit(solution)/shard_map/scatter | solution.py:55
  61.4 9.4 %pad_maximum_fusion = bf16[128,2,7168]{2,1,0:T(2,128)(2,1)} fusion(bf16[128,1,7168]{2,1,0:T(2,128)(2,1)S(1)} %copy.71, bf16[128,1,7168]{2,1,0:T(2,128)(2,1)S(1)} %copy.70), kind=kLoop, calls=%fused_computation.33 | loop fusion | flops 7340032 | bytes 7340032 | tf_op jit(solution)/shard_map/stack | solution.py:94
  70.8 32.3 %gather_fusion.2 = bf16[384,2,7168]{2,1,0:T(2,128)(2,1)} fusion(bf16[128,2,7168]{2,1,0:T(2,128)(2,1)} %pad_maximum_fusion, s32[1024]{0:T(1024)S(1)} %pad_clamp_fusion), kind=kCustom, calls=%fused_computation.2 | custom fusion | bytes 22021632 | tf_op jit(solution)/shard_map/gather | solution.py:58
  103.1 12.2 %copy_select_fusion = bf16[4,96,2,7168]{3,1,2,0:T(8,128)(2,1)} fusion(bf16[4,96,2,7168]{3,2,1,0:T(2,128)(2,1)} %bitcast.121, pred[4,96]{1,0:T(4,128)(4,1)S(1)} %broadcast_compare_fusion), kind=kLoop, calls=%fused_computation.7 | loop fusion | flops 5505024 | bytes 22020480 | tf_op jit(solution)/shard_map/jit(_where)/select_n | solution.py:58
  115.4 42.7 %all-to-all-done = bf16[4,96,1,7168]{3,1,2,0:T(8,128)(2,1)} async-done(((bf16[4,96,1,7168]{3,1,2,0:T(8,128)(2,1)}), bf16[4,96,1,7168]{3,1,2,0:T(8,128)(2,1)}, u32[]{:S(2)}, u32[]{:S(2)}) %all-to-all-start) | async-done | bytes 5505056 | tf_op jit(solution)/shard_map/all_to_all | solution.py:60
  158.1 9.2 %all-to-all-start.2 = ((bf16[4,96,2,7168]{3,1,2,0:T(8,128)(2,1)}), bf16[4,96,2,7168]{3,1,2,0:T(8,128)(2,1)}, u32[]{:S(2)}, u32[]{:S(2)}) async-start(bf16[4,96,2,7168]{3,1,2,0:T(8,128)(2,1)} %copy_select_fusion), calls=%async_computation.2 | async-start | bytes 22020096 | tf_op jit(solution)/shard_map/all_to_all | solution.py:60
  175.1 8.1 convolution_convert_fusion.1
  183.2 219.8 %all-to-all-done.2 = bf16[4,96,2,7168]{3,1,2,0:T(8,128)(2,1)} async-done(((bf16[4,96,2,7168]{3,1,2,0:T(8,128)(2,1)}), bf16[4,96,2,7168]{3,1,2,0:T(8,128)(2,1)}, u32[]{:S(2)}, u32[]{:S(2)}) %all-to-all-start.2) | async-done | bytes 11010080 | tf_op jit(solution)/shard_map/all_to_all | solution.py:60
  403.0 8.4 all-to-all-start.1
  426.2 9.8 %convolution_convert_fusion = bf16[4,96,7168]{2,1,0:T(8,128)(2,1)} fusion(bf16[4,96,512]{2,1,0:T(8,128)(2,1)S(1)} %fusion.21, bf16[1,1,7168,512]{3,2,1,0:T(8,128)(2,1)} %param.20), kind=kOutput, calls=%fused_computation.8 | convolution fusion | flops 2821324800 | bytes 13238272 | tf_op jit(solution)/shard_map/sch,dh->scd/dot_general | solution.py:40
  436.1 93.0 %all-to-all-done.1 = bf16[4,96,7168]{2,1,0:T(8,128)(2,1)} async-done(((bf16[4,96,7168]{2,1,0:T(8,128)(2,1)}), bf16[4,96,7168]{2,1,0:T(8,128)(2,1)}, u32[]{:S(2)}, u32[]{:S(2)}) %all-to-all-start.1) | async-done | bytes 5505056 | tf_op jit(solution)/shard_map/all_to_all | solution.py:64
  529.1 8.1 all-to-all-start.3
  539.0 11.0 %gather_fusion.1 = bf16[256,7168]{1,0:T(8,128)(2,1)} fusion(bf16[4,96,7168]{2,1,0:T(8,128)(2,1)} %all-to-all-done.1, s32[256]{0:T(256)S(1)} %bitcast.123), kind=kCustom, calls=%fused_computation.1 | custom fusion | bytes 7342080 | tf_op jit(solution)/shard_map/gather | solution.py:65
  550.0 8.6 reshape.190
  558.6 138.5 %all-to-all-done.3 = bf16[4,96,7168]{2,1,0:T(8,128)(2,1)} async-done(((bf16[4,96,7168]{2,1,0:T(8,128)(2,1)}), bf16[4,96,7168]{2,1,0:T(8,128)(2,1)}, u32[]{:S(2)}, u32[]{:S(2)}) %all-to-all-start.3) | async-done | bytes 5505056 | tf_op jit(solution)/shard_map/all_to_all | solution.py:64
  697.1 11.0 %gather_fusion.3 = bf16[256,7168]{1,0:T(8,128)(2,1)} fusion(bf16[4,96,7168]{2,1,0:T(8,128)(2,1)} %all-to-all-done.3, s32[256]{0:T(256)S(1)} %bitcast.124), kind=kCustom, calls=%fused_computation.3 | custom fusion | bytes 7342080 | tf_op jit(solution)/shard_map/gather | solution.py:65
  708.1 8.3 reshape.193
  723.8 8.4 convert_bitcast_fusion.1
  732.2 21.5 %all-reduce.3.cloned.1.call-done = (bf16[128,2,7168]{2,1,0:T(2,128)(2,1)}, bf16[128,2,7168]{2,1,0:T(2,128)(2,1)}) async-done(((bf16[128,2,7168]{2,1,0:T(2,128)(2,1)}, bf16[128,2,7168]{2,1,0:T(2,128)(2,1)}), (bf16[128,2,7168]{2,1,0:T(2,128)(2,1)}, bf16[128,2,7168]{2,1,0:T(2,128)(2,1)})) %all-reduce.3.cloned.1.call-update) | async-done | bytes 7340048 | tf_op jit(solution)/shard_map/psum | solution.py:66
  753.7 11.4 %multiply_reduce_fusion.1 = f32[128,7168]{1,0:T(8,128)S(1)} fusion(bf16[128,2,7168]{2,1,0:T(2,128)(2,1)} %get-tuple-element.4, f32[128,2]{1,0:T(8,128)S(1)} %copy.57), kind=kLoop, calls=%fused_computation.19 | loop fusion | flops 4587520 | bytes 7341056 | tf_op jit(solution)/shard_map/reduce_sum | solution.py:68
  770.0 10.3 %multiply_reduce_fusion = f32[128,7168]{1,0:T(8,128)S(1)} fusion(bf16[128,2,7168]{2,1,0:T(2,128)(2,1)S(1)} %copy-done.3, f32[128,2]{1,0:T(8,128)S(1)} %copy.64), kind=kLoop, calls=%fused_computation.18 | loop fusion | flops 4587520 | bytes 7341056 | tf_op jit(solution)/shard_map/reduce_sum | solution.py:68
  785.6 13.2 %select_reduce_fusion = f32[16]{0:T(128)S(1)} fusion(pred[1024,1024]{1,0:T(8,128)(4,1)S(1)} %iota_compare_fusion, bf16[128,16,8,128]{3,2,1,0:T(8,128)(2,1)S(1)} %copy-done.7, bf16[128,16,8,128]{3,2,1,0:T(8,128)(2,1)S(1)} %copy-done.8), kind=kOutput, calls=%fused_computation.6 | convolution fusion | flops 4345298944 | bytes 9437248 | tf_op jit(solution)/shard_map/qhd,khd->hqk/dot_general | solution.py:117
  810.5 40.1 %collective-permute-done.1 = bf16[128,7168]{1,0:T(8,128)(2,1)S(1)} collective-permute-done((bf16[128,7168]{1,0:T(8,128)(2,1)}, bf16[128,7168]{1,0:T(8,128)(2,1)S(1)}, u32[]{:S(2)}, u32[]{:S(2)}) %collective-permute-start.1) | collective-permute-done | bytes 1835040 | tf_op jit(solution)/shard_map/ppermute | solution.py:16
  (91 shorter events, 88.0 us)
Async XLA Ops:
  8.0 14.6 %copy-start = (bf16[1,128,7168]{2,1,0:T(8,128)(2,1)S(1)}, bf16[1,128,7168]{2,1,0:T(8,128)(2,1)}, u32[]{:S(2)}) copy-start(bf16[1,128,7168]{2,1,0:T(8,128)(2,1)} %param.13) | copy-start | bytes 5505028
  34.5 5.8 copy-start.4
  34.5 123.6 %all-to-all-start = ((bf16[4,96,1,7168]{3,1,2,0:T(8,128)(2,1)}), bf16[4,96,1,7168]{3,1,2,0:T(8,128)(2,1)}, u32[]{:S(2)}, u32[]{:S(2)}) async-start(bf16[4,96,1,7168]{3,1,2,0:T(8,128)(2,1)} %broadcast_select_fusion), calls=%async_computation | async-start | bytes 11010048 | tf_op jit(solution)/shard_map/all_to_all | solution.py:60
  54.1 4.5 copy-start.1
  158.1 244.9 %all-to-all-start.2 = ((bf16[4,96,2,7168]{3,1,2,0:T(8,128)(2,1)}), bf16[4,96,2,7168]{3,1,2,0:T(8,128)(2,1)}, u32[]{:S(2)}, u32[]{:S(2)}) async-start(bf16[4,96,2,7168]{3,1,2,0:T(8,128)(2,1)} %copy_select_fusion), calls=%async_computation.2 | async-start | bytes 22020096 | tf_op jit(solution)/shard_map/all_to_all | solution.py:60
  403.0 126.1 %all-to-all-start.1 = ((bf16[4,96,7168]{2,1,0:T(8,128)(2,1)}), bf16[4,96,7168]{2,1,0:T(8,128)(2,1)}, u32[]{:S(2)}, u32[]{:S(2)}) async-start(bf16[4,96,7168]{2,1,0:T(8,128)(2,1)} %convolution_convert_fusion.1), calls=%async_computation.1 | async-start | bytes 11010048 | tf_op jit(solution)/shard_map/all_to_all | solution.py:64
  529.1 168.0 %all-to-all-start.3 = ((bf16[4,96,7168]{2,1,0:T(8,128)(2,1)}), bf16[4,96,7168]{2,1,0:T(8,128)(2,1)}, u32[]{:S(2)}, u32[]{:S(2)}) async-start(bf16[4,96,7168]{2,1,0:T(8,128)(2,1)} %convolution_convert_fusion), calls=%async_computation.3 | async-start | bytes 11010048 | tf_op jit(solution)/shard_map/all_to_all | solution.py:64
  537.3 180.4 %all-gather.7.cloned.1.call-start = ((), (), s32[]{:S(2)}) async-start(), calls=%async_computation.5 | async-start | bytes 1310720 | tf_op jit(solution)/shard_map/all_gather | solution.py:111
  538.0 185.8 %all-gather.5.cloned.1.call-start = ((), (), s32[]{:S(2)}) async-start(), calls=%async_computation.4 | async-start | bytes 1966080 | tf_op jit(solution)/shard_map/all_gather | solution.py:103
  538.7 215.0 %all-reduce.3.cloned.1.call-start = ((), (), s32[]{:S(2)}) async-start(), calls=%async_computation.6 | async-start | bytes 14680064 | tf_op jit(solution)/shard_map/psum | solution.py:66
  716.4 0.7 copy-start.5
  716.4 0.8 copy-start.6
  765.2 4.8 copy-start.3
  766.8 13.6 %copy-start.2 = (bf16[1,128,7168]{2,1,0:T(8,128)(2,1)S(1)}, bf16[1,128,7168]{2,1,0:T(8,128)(2,1)}, u32[]{:S(2)}) copy-start(bf16[1,128,7168]{2,1,0:T(8,128)(2,1)} %param.17) | copy-start | bytes 5505028
  766.8 43.7 %collective-permute-start = (bf16[128,7168]{1,0:T(8,128)(2,1)}, bf16[128,7168]{1,0:T(8,128)(2,1)}, u32[]{:S(2)}, u32[]{:S(2)}) collective-permute-start(bf16[128,7168]{1,0:T(8,128)(2,1)} %fusion.14), channel_id=1, source_target_pairs={{0,8},{8,16},{16,24},{1,9},{9,17},{17,25},{2,10},{10,18},{18,26},{... | collective-permute-start | bytes 5505032 | tf_op jit(solution)/shard_map/ppermute | solution.py:16
  770.0 15.6 %copy-start.8 = (bf16[128,16,8,128]{3,2,1,0:T(8,128)(2,1)S(1)}, bf16[128,16,8,128]{3,2,1,0:T(8,128)(2,1)}, u32[]{:S(2)}) copy-start(bf16[128,16,8,128]{3,2,1,0:T(8,128)(2,1)} %convert_bitcast_fusion.1) | copy-start | bytes 12582916
  780.4 5.2 copy-start.7
  782.0 68.7 %collective-permute-start.1 = (bf16[128,7168]{1,0:T(8,128)(2,1)}, bf16[128,7168]{1,0:T(8,128)(2,1)S(1)}, u32[]{:S(2)}, u32[]{:S(2)}) collective-permute-start(bf16[128,7168]{1,0:T(8,128)(2,1)} %fusion.13), channel_id=1, source_target_pairs={{8,0},{16,8},{24,16},{9,1},{17,9},{25,17},{10,2},{18,10},{26,18},{... | collective-permute-start | bytes 5505032 | tf_op jit(solution)/shard_map/ppermute | solution.py:16
Sparse Core Ops, SparseCore 0:
  539.7 55.0 all-gather.6
  596.4 80.5 all-gather.4
Sparse Core Ops, SparseCore 1:
  716.5 37.2 all-reduce.2
where the time goes:
time: 869 us; the launch traced here: 862 us
  waiting for transfers between devices  558 us (64%)
  local copies, waits for them, and re-layouts  115 us (13%)
  matrix products  68.4 us (8%)
  other arithmetic  63 us (7%)
  starting transfers between devices  38.7 us (4%)
  between operations  16 us (2%)
    all_to_all x2, waiting for transfers between devices, route_through(): lax.all_to_all(outgoing, 'expert', split_axis=0, concat_axis=0, tiled=True)  262 us
    all_to_all x2, waiting for transfers between devices, route_through(): lax.all_to_all(pieces, 'expert', split_axis=0, concat_axis=0, tiled=True)  232 us
    ppermute x2, waiting for transfers between devices, shifted(): return lax.ppermute(block, axis, route)  40.9 us
    gather x2, local copies, waits for them, and re-layouts, route_through(): stacked[source]  38.8 us
    scatter x2, local copies, waits for them, and re-layouts, route_through(): slot_table.at[flat_ids, slot_rank]  22.9 us
    gather x2, local copies, waits for them, and re-layouts, route_through(): picked = returned[flat_ids, slot_rank].astype(jnp.float32)  21.9 us
    reduce_sum x2, other arithmetic, route_through(): return jnp.sum(gate_vals[:, :, None] * routed, axis=1)  21.8 us
    psum x1, waiting for transfers between devices, route_through(): routed = lax.psum(picked.astype(jnp.bfloat16), 'dp')  21.5 us
  transfers between devices with their start and end apart: 9, of which 7 were waited for; matrix products, arithmetic and copies ran while one was open for 24% of the time, Pallas kernels for 0%

commit v1 on v0

v1 whole, which is shorter than its diff:
```python
import jax
import jax.numpy as jnp
from jax import lax
from jax.sharding import PartitionSpec as P

HD = 128

clip_limit = 100.0
logit_scale = 192.0 ** (-0.5)


def silu_grad(pre_act):
    sigmoid_val = jax.nn.sigmoid(pre_act)
    return sigmoid_val * (1.0 + pre_act * (1.0 - sigmoid_val))


def swap(block):
    return lax.ppermute(block, "dp", [(0, 1), (1, 0)])


def own_half(array, axis, core):
    width = array.shape[axis] // 2
    return lax.dynamic_slice_in_dim(array, core * width, width, axis)


def other_half(array, axis, core):
    width = array.shape[axis] // 2
    return lax.dynamic_slice_in_dim(array, (1 - core) * width, width, axis)


def after(block, *earlier):
    return lax.optimization_barrier((block,) + earlier)[0]


def shifted(block, axis, distance):
    devices = range(lax.axis_size(axis))
    route = [(i - distance, i) for i in devices if i - distance in devices]
    return lax.ppermute(block, axis, route)


def spread(block, place):
    n = lax.axis_size("expert")
    up, down = [block], [block]
    for step in range(1, n):
        up.append(lax.ppermute(up[-1], "expert", [(j, j + 1) for j in range(step - 1, n - 1)]))
        down.append(lax.ppermute(down[-1], "expert", [(j, j - 1) for j in range(1, n - step + 1)]))
    blocks = [block] + [jnp.where(place >= r, up[r], down[n - r]) for r in range(1, n)]
    return blocks, (up[min(2, n - 1)], down[min(2, n - 1)])


def collect(parts):
    n = lax.axis_size("expert")
    up = down = None
    for step in range(1, n):
        first, second = parts[step], parts[n - step]
        if up is not None:
            first, second = first + up, second + down
        up = lax.ppermute(first.astype(jnp.bfloat16), "expert", [(j, j + 1) for j in range(0, min(step, n - 1))])
        down = lax.ppermute(
            second.astype(jnp.bfloat16), "expert", [(j, j - 1) for j in range(max(n - step, 1), n)]
        )
        up, down = up.astype(jnp.float32), down.astype(jnp.float32)
    return parts[0] + up + down


def coefficients(routes, gates, place):
    n = lax.axis_size("expert")
    result = []
    for r in range(n):
        target = lax.rem(place + r, n)
        value = jnp.sum(jnp.where(routes == target, gates, 0.0), axis=-1)
        if r:
            value = lax.ppermute(value, "expert", [(j, (j + r) % n) for j in range(n)])
        result.append(value)
    return result


def times(rows, weight):
    return jnp.dot(rows, weight, preferred_element_type=jnp.float32)


def times_transposed(rows, weight):
    return lax.dot_general(rows, weight, (((1,), (1,)), ((), ())), preferred_element_type=jnp.float32)


def on_device(
    fwd_tokens,
    fwd_routes,
    fwd_gates,
    bwd_saved,
    bwd_grads,
    bwd_routes,
    bwd_gates,
    w_up,
    w_down,
    query_latent,
    key_latent,
    query_weight,
    key_weight,
):
    n = lax.axis_size("expert")
    place = lax.axis_index("expert")
    core = lax.axis_index("dp")
    tok = fwd_tokens.shape[1]

    tokens_half = own_half(fwd_tokens[0], 1, core)
    saved_half = own_half(bwd_saved[0], 1, core)
    grads_half = own_half(bwd_grads[0], 1, core)
    routes = jnp.stack([fwd_routes[0], bwd_routes[0]])
    gates = jnp.stack([fwd_gates[0], bwd_gates[0]])
    latent = jnp.concatenate([query_latent[0, 0], key_latent[0, 0]], axis=1)

    tokens_all, mark = spread(tokens_half, place)
    up_own = own_half(w_up[0, 0], 0, core)
    up_other = swap(other_half(w_up[0, 0], 0, core))
    down_own = own_half(w_down[0, 0], 1, core)
    down_other = swap(other_half(w_down[0, 0], 1, core))
    coef = coefficients(routes, gates, place)
    saved_all, mark = spread(after(saved_half, *mark), place)
    grads_all, mark = spread(after(grads_half, *mark), place)
    latent_all, mark = spread(after(latent, *mark), place)

    rows = jnp.concatenate(tokens_all, axis=0)
    pre_act = times(rows, up_own) + swap(times(rows, up_other))
    hidden = jax.nn.silu(pre_act).astype(jnp.bfloat16)
    out = times(hidden, down_own) + times(swap(hidden), down_other)
    parts = [out[r * tok:(r + 1) * tok] * coef[r][0][:, None] for r in range(n)]
    section_half = (tokens_half.astype(jnp.float32) + collect(parts)).astype(jnp.bfloat16)
    fwd_half = shifted(section_half, "pipe", 1)

    rows = jnp.concatenate(saved_all, axis=0)
    pre_act = times(rows, up_own) + swap(times(rows, up_other))
    rows = jnp.concatenate(grads_all, axis=0)
    back = times_transposed(rows, down_own) + swap(times_transposed(rows, down_other))
    pre_grad = (back * silu_grad(pre_act)).astype(jnp.bfloat16)
    out = times_transposed(pre_grad, up_own) + times_transposed(swap(pre_grad), up_other)
    parts = [out[r * tok:(r + 1) * tok] * coef[r][1][:, None] for r in range(n)]
    grad_half = (grads_half.astype(jnp.float32) + collect(parts)).astype(jnp.bfloat16)
    bwd_half = shifted(grad_half, "pipe", -1)

    query_proj = query_weight[0]
    key_proj = key_weight[0]
    heads_here = query_proj.shape[1] // HD
    latents = jnp.concatenate(latent_all, axis=0)
    seq_len = latents.shape[0]
    per = seq_len // n
    owners = lax.rem(place - jnp.arange(n, dtype=jnp.int32) + n, n)
    pos = (owners[:, None] * per + jnp.arange(per, dtype=jnp.int32)[None, :]).reshape(-1)
    rank = query_proj.shape[0]
    queries = times(latents[:, :rank], query_proj).astype(jnp.bfloat16).reshape(seq_len, heads_here, HD)
    keys = times(latents[:, rank:], key_proj).astype(jnp.bfloat16).reshape(seq_len, heads_here, HD)
    scores = jnp.einsum("qhd,khd->hqk", queries, keys, preferred_element_type=jnp.float32) * logit_scale
    scores = jnp.where((pos[:, None] >= pos[None, :])[None], scores, -1e30)
    local_max = jnp.max(scores, axis=(1, 2))
    head_max = jnp.maximum(local_max, swap(local_max))
    factor = jnp.sqrt(clip_limit / jnp.maximum(head_max, clip_limit))
    col_factor = jnp.repeat(factor, HD)
    query_clipped = (query_proj.astype(jnp.float32) * col_factor[None, :]).astype(jnp.bfloat16)
    key_clipped = (key_proj.astype(jnp.float32) * col_factor[None, :]).astype(jnp.bfloat16)

    def whole(half):
        theirs = swap(half)
        first = jnp.where(core == 0, half, theirs)
        second = jnp.where(core == 0, theirs, half)
        return jnp.concatenate([first, second], axis=1)

    return (whole(fwd_half)[None], whole(bwd_half)[None], query_clipped[None], key_clipped[None])


def solution(mesh):
    rows3 = P("pipe", "expert", None)
    in_specs = (rows3,) * 7 + (
        P("pipe", "expert", None, "dp"),
        P("pipe", "expert", "dp", None),
        P("pipe", "dp", "expert", None),
        P("pipe", "dp", "expert", None),
        P("pipe", None, "expert"),
        P("pipe", None, "expert"),
    )
    out_specs = (rows3, rows3, P("pipe", None, "expert"), P("pipe", None, "expert"))
    return jax.shard_map(
        on_device, mesh=mesh, in_specs=in_specs, out_specs=out_specs, check_vma=False
    )
```

time: 869 us -> 436 us (0.50)
  waiting for transfers between devices: 558 us -> 179 us
  starting transfers between devices: 38.7 us -> 144 us
  local copies, waits for them, and re-layouts: 115 us -> 15.5 us
  other arithmetic: 63 us -> 29.4 us
  between operations: 16 us -> 1.66 us
    all_to_all x4 -> x0, waiting for transfers between devices: 494 us -> none  [the longest x2 262 us: route_through(): lax.all_to_all(outgoing, 'expert', split_axis=0, concat_axis=0, tiled=True)]
    ppermute x0 -> x49, waiting for transfers between devices: none -> 166 us  [the longest x12 88.2 us: spread(): lax.ppermute(up[-1], 'expert', [(j, j + 1) for j in range(step - 1, n - 1)])]
    ppermute x0 -> x49, starting transfers between devices: none -> 139 us  [the longest x12 36.3 us: spread(): lax.ppermute(up[-1], 'expert', [(j, j + 1) for j in range(step - 1, n - 1)])]
    gather x4 -> x0, local copies, waits for them, and re-layouts: 60.7 us -> none  [the longest x2 38.8 us: route_through(): stacked[source]]
    all_to_all x4 -> x0, starting transfers between devices: 31.6 us -> none  [the longest x2 16.6 us: route_through(): lax.all_to_all(pieces, 'expert', split_axis=0, concat_axis=0, tiled=True)]
    ppermute x2, waiting for transfers between devices: 40.9 us -> 12.8 us  [shifted(): return lax.ppermute(block, axis, route)]
    scatter x2 -> x0, local copies, waits for them, and re-layouts: 22.9 us -> none  [route_through(): slot_table.at[flat_ids, slot_rank]]
    psum x1 -> x0, waiting for transfers between devices: 21.5 us -> none  [route_through(): routed = lax.psum(picked.astype(jnp.bfloat16), 'dp')]
  transfers between devices with their start and end apart: 9 -> 51, of which waited for: 7 -> 18; matrix products, arithmetic and copies ran while one was open for 24% -> 23% of each run, Pallas kernels for 0% -> 0%
where the time goes in v1:
time: 436 us; the launch traced here: 433 us
  waiting for transfers between devices  179 us (41%)
  starting transfers between devices  144 us (33%)
  matrix products  63.5 us (15%)
  other arithmetic  29.4 us (7%)
  local copies, waits for them, and re-layouts  15.5 us (4%)
    ppermute x12, waiting for transfers between devices, spread(): lax.ppermute(up[-1], 'expert', [(j, j + 1) for j in range(step - 1, n - 1)])  88.2 us
    ppermute x6, waiting for transfers between devices, collect(): lax.ppermute(second.astype(jnp.bfloat16), 'expert', [(j, j - 1) for j in...  43.1 us
    ppermute x12, starting transfers between devices, spread(): lax.ppermute(up[-1], 'expert', [(j, j + 1) for j in range(step - 1, n - 1)])  36.3 us
    dot_general x8, matrix products, times(): return jnp.dot(rows, weight, preferred_element_type=jnp.float32)  34.3 us
    ppermute x12, starting transfers between devices, spread(): lax.ppermute(down[-1], 'expert', [(j, j - 1) for j in range(1, n - step +...  32.3 us
    ppermute x10, starting transfers between devices, swap(): return lax.ppermute(block, 'dp', [(0, 1), (1, 0)])  29.9 us
    ppermute x6, starting transfers between devices, collect(): lax.ppermute(second.astype(jnp.bfloat16), 'expert', [(j, j - 1) for j in...  27 us
    ppermute x3, waiting for transfers between devices, coefficients(): value = lax.ppermute(value, 'expert', [(j, (j + r) % n) for j in range(n)])  18.7 us
  transfers between devices with their start and end apart: 51, of which 18 were waited for; matrix products, arithmetic and copies ran while one was open for 23% of the time, Pallas kernels for 0%

profile of v1, /device:TPU:19, one launch (start us, length us, event | category | flops | bytes accessed | tf_op | source)
XLA Modules:
  0.0 433.3 jit_solution(18332308295779128857)
XLA Ops:
  34.5 16.3 %collective-permute-done.11 = f32[2,128]{1,0:T(2,128)S(1)} collective-permute-done((f32[2,128]{1,0:T(2,128)S(1)}, f32[2,128]{1,0:T(2,128)S(1)}, u32[]{:S(2)}, u32[]{:S(2)}) %collective-permute-start.11) | collective-permute-done | bytes 1056 | tf_op jit(solution)/shard_map/ppermute | solution.py:73
  53.2 4.5 %collective-permute-start.21 = (bf16[128,3584]{1,0:T(8,128)(2,1)}, bf16[128,3584]{1,0:T(8,128)(2,1)S(1)}, u32[]{:S(2)}, u32[]{:S(2)}) collective-permute-start(bf16[128,3584]{1,0:T(8,128)(2,1)} %dynamic-slice_bitcast_fusion.2), channel_id=1, source_target_pairs={{0,1},{1,2},{2,3},{4,5},{5,6},{6,7},{8,9},{9,10},{10,11},{12,13},{... | collective-permute-start | bytes 2752520 | tf_op jit(solution)/shard_map/ppermute | solution.py:45
  64.4 29.0 %collective-permute-done.5 = bf16[128,3584]{1,0:T(8,128)(2,1)S(1)} collective-permute-done((bf16[128,3584]{1,0:T(8,128)(2,1)}, bf16[128,3584]{1,0:T(8,128)(2,1)S(1)}, u32[]{:S(2)}, u32[]{:S(2)}) %collective-permute-start.5) | collective-permute-done | bytes 917536 | tf_op jit(solution)/shard_map/ppermute | solution.py:45
  102.3 10.7 %collective-permute-done.22 = bf16[128,3584]{1,0:T(8,128)(2,1)S(1)} collective-permute-done((bf16[128,3584]{1,0:T(8,128)(2,1)S(1)}, bf16[128,3584]{1,0:T(8,128)(2,1)S(1)}, u32[]{:S(2)}, u32[]{:S(2)}) %collective-permute-start.22) | collective-permute-done | bytes 917536 | tf_op jit(solution)/shard_map/ppermute | solution.py:45
  120.0 4.4 %fusion.58 = f32[512,512]{1,0:T(8,128)S(1)} fusion(bf16[3584,512]{1,0:T(8,128)(2,1)} %collective-permute-done.6, bf16[128,3584]{1,0:T(8,128)(2,1)S(1)} %broadcast_select_fusion.2, bf16[128,3584]{1,0:T(8,128)(2,1)S(1)} %broadcast_select_fusion.5, bf16[128,3584]{1,0:T(8,128)(2,1)S(1)} %broadcast_select_fusion.8, bf16[128,3584]{1,0:T(8,128)(2,1)} %dynamic-slice_bitcast_fusion.4), kind=kOutput, calls=%fused_computation.99 | convolution fusion | flops 1893728256 | bytes 8388608 | tf_op jit(solution)/shard_map/dot_general | solution.py:79
  124.4 6.4 %collective-permute-start.7 = (f32[512,512]{1,0:T(8,128)S(1)}, f32[512,512]{1,0:T(8,128)S(1)}, u32[]{:S(2)}, u32[]{:S(2)}) collective-permute-start(f32[512,512]{1,0:T(8,128)S(1)} %fusion.58), channel_id=1, source_target_pairs={{0,4},{4,0},{1,5},{5,1},{2,6},{6,2},{3,7},{7,3},{8,12},{12,8},{9,1... | collective-permute-start | bytes 3145736 | tf_op jit(solution)/shard_map/ppermute | solution.py:18
  134.0 20.0 %collective-permute-done.33 = bf16[128,3584]{1,0:T(8,128)(2,1)S(1)} collective-permute-done((bf16[128,3584]{1,0:T(8,128)(2,1)S(1)}, bf16[128,3584]{1,0:T(8,128)(2,1)S(1)}, u32[]{:S(2)}, u32[]{:S(2)}) %collective-permute-start.33) | collective-permute-done | bytes 917536 | tf_op jit(solution)/shard_map/ppermute | solution.py:45
  163.0 5.1 %fusion.56 = f32[512,512]{1,0:T(8,128)} fusion(bf16[3584,512]{1,0:T(8,128)(2,1)} %collective-permute-done.6, bf16[128,3584]{1,0:T(8,128)(2,1)S(1)} %broadcast_select_fusion, bf16[128,3584]{1,0:T(8,128)(2,1)S(1)} %broadcast_select_fusion.3, bf16[128,3584]{1,0:T(8,128)(2,1)S(1)} %broadcast_select_fusion.6, bf16[128,3584]{1,0:T(8,128)(2,1)S(1)} %copy-done.11), kind=kOutput, calls=%fused_computation.97 | convolution fusion | flops 1893728256 | bytes 8388608 | tf_op jit(solution)/shard_map/dot_general | solution.py:79
  181.7 11.0 %collective-permute-done.29 = bf16[128,3584]{1,0:T(8,128)(2,1)S(1)} collective-permute-done((bf16[128,3584]{1,0:T(8,128)(2,1)S(1)}, bf16[128,3584]{1,0:T(8,128)(2,1)S(1)}, u32[]{:S(2)}, u32[]{:S(2)}) %collective-permute-start.29) | collective-permute-done | bytes 917536 | tf_op jit(solution)/shard_map/ppermute | solution.py:45
  202.4 5.4 %fusion.35 = f32[512,512]{1,0:T(8,128)} fusion(f32[512,512]{1,0:T(8,128)} %collective-permute-done.34, bf16[1,1,7168,512]{3,2,1,0:T(8,128)(2,1)} %param.20, s32[]{:T(128)S(6)} %select_n.111, bf16[128,3584]{1,0:T(8,128)(2,1)S(1)} %copy-done.17, bf16[128,3584]{1,0:T(8,128)(2,1)S(1)} %copy-done.15, bf16[128,3584]{1,0:T(8,128)(2,1)S(1)} %copy-done.19, ...), kind=kOutput, calls=%fused_computation.65 | convolution fusion | flops 1893990400 | bytes 9437188 | tf_op jit(solution)/shard_map/dot_general | solution.py:79
  213.6 10.4 %collective-permute-start.46 = (bf16[256,1280]{1,0:T(8,128)(2,1)S(1)}, bf16[256,1280]{1,0:T(8,128)(2,1)S(1)}, u32[]{:S(2)}, u32[]{:S(2)}) collective-permute-start(bf16[256,1280]{1,0:T(8,128)(2,1)S(1)} %collective-permute-done.45), channel_id=1, source_target_pairs={{1,0},{2,1},{5,4},{6,5},{9,8},{10,9},{13,12},{14,13},{17,16},{18,1... | collective-permute-start | bytes 1966088 | tf_op jit(solution)/shard_map/ppermute | solution.py:46
  224.0 4.4 %collective-permute-done.30 = bf16[128,3584]{1,0:T(8,128)(2,1)S(1)} collective-permute-done((bf16[128,3584]{1,0:T(8,128)(2,1)S(1)}, bf16[128,3584]{1,0:T(8,128)(2,1)S(1)}, u32[]{:S(2)}, u32[]{:S(2)}) %collective-permute-start.30) | collective-permute-done | bytes 917536 | tf_op jit(solution)/shard_map/ppermute | solution.py:45
  236.6 8.2 %collective-permute-done.48 = bf16[256,1280]{1,0:T(8,128)(2,1)} collective-permute-done((bf16[256,1280]{1,0:T(8,128)(2,1)S(1)}, bf16[256,1280]{1,0:T(8,128)(2,1)}, u32[]{:S(2)}, u32[]{:S(2)}) %collective-permute-start.48) | collective-permute-done | bytes 655392 | tf_op jit(solution)/shard_map/ppermute | solution.py:45
  251.1 4.9 %collective-permute-start.15 = (bf16[128,3584]{1,0:T(8,128)(2,1)S(1)}, bf16[128,3584]{1,0:T(8,128)(2,1)}, u32[]{:S(2)}, u32[]{:S(2)}) collective-permute-start(bf16[128,3584]{1,0:T(8,128)(2,1)S(1)} %get-tuple-element.16), channel_id=1, source_target_pairs={{0,1},{1,2},{2,3},{4,5},{5,6},{6,7},{8,9},{9,10},{10,11},{12,13},{... | collective-permute-start | bytes 2752520 | tf_op jit(solution)/shard_map/ppermute | solution.py:58
  280.0 4.9 %convert_bitcast_fusion.1 = bf16[128,16,8,128]{3,2,1,0:T(8,128)(2,1)} fusion(bf16[1,768,2048]{2,1,0:T(8,128)(2,1)S(1)} %copy-done.4, bf16[1024,1280]{1,0:T(8,128)(2,1)S(1)} %pad_maximum_fusion.3), kind=kOutput, calls=%fused_computation.10 | convolution fusion | flops 3223322624 | bytes 8912896 | tf_op jit(solution)/shard_map/dot_general | solution.py:79
  288.1 16.5 %collective-permute-start.17 = (bf16[128,3584]{1,0:T(8,128)(2,1)S(1)}, bf16[128,3584]{1,0:T(8,128)(2,1)S(1)}, u32[]{:S(2)}, u32[]{:S(2)}) collective-permute-start(bf16[128,3584]{1,0:T(8,128)(2,1)S(1)} %add_convert_fusion.5), channel_id=1, source_target_pairs={{2,1},{3,2},{6,5},{7,6},{10,9},{11,10},{14,13},{15,14},{18,17},{19... | collective-permute-start | bytes 2752520 | tf_op jit(solution)/shard_map/ppermute | solution.py:59
  304.5 13.4 %collective-permute-done.37 = bf16[128,3584]{1,0:T(8,128)(2,1)S(1)} collective-permute-done((bf16[128,3584]{1,0:T(8,128)(2,1)S(1)}, bf16[128,3584]{1,0:T(8,128)(2,1)S(1)}, u32[]{:S(2)}, u32[]{:S(2)}) %collective-permute-start.37) | collective-permute-done | bytes 917536 | tf_op jit(solution)/shard_map/ppermute | solution.py:58
  324.7 13.8 %collective-permute-done.39 = bf16[128,3584]{1,0:T(8,128)(2,1)S(1)} collective-permute-done((bf16[128,3584]{1,0:T(8,128)(2,1)S(1)}, bf16[128,3584]{1,0:T(8,128)(2,1)S(1)}, u32[]{:S(2)}, u32[]{:S(2)}) %collective-permute-start.39) | collective-permute-done | bytes 917536 | tf_op jit(solution)/shard_map/ppermute | solution.py:59
  340.8 17.4 %collective-permute-done.18 = bf16[128,3584]{1,0:T(8,128)(2,1)S(1)} collective-permute-done((bf16[128,3584]{1,0:T(8,128)(2,1)S(1)}, bf16[128,3584]{1,0:T(8,128)(2,1)S(1)}, u32[]{:S(2)}, u32[]{:S(2)}) %collective-permute-start.18) | collective-permute-done | bytes 917536 | tf_op jit(solution)/shard_map/ppermute | solution.py:59
  366.1 11.9 %collective-permute-done.40 = bf16[128,3584]{1,0:T(8,128)(2,1)S(1)} collective-permute-done((bf16[128,3584]{1,0:T(8,128)(2,1)S(1)}, bf16[128,3584]{1,0:T(8,128)(2,1)S(1)}, u32[]{:S(2)}, u32[]{:S(2)}) %collective-permute-start.40) | collective-permute-done | bytes 917536 | tf_op jit(solution)/shard_map/ppermute | solution.py:59
  381.3 12.8 %select_reduce_fusion = f32[16]{0:T(128)S(1)} fusion(pred[1024,1024]{1,0:T(8,128)(4,1)S(1)} %broadcast_compare_fusion, bf16[128,16,8,128]{3,2,1,0:T(8,128)(2,1)S(1)} %copy-done.26, bf16[128,16,8,128]{3,2,1,0:T(8,128)(2,1)} %convert_bitcast_fusion.1), kind=kOutput, calls=%fused_computation | convolution fusion | flops 4345298944 | bytes 9437248 | tf_op jit(solution)/shard_map/qhd,khd->hqk/dot_general | solution.py:152
  394.1 5.3 %collective-permute-start.50 = (f32[16]{0:T(128)S(1)}, f32[16]{0:T(128)S(1)}, u32[]{:S(2)}, u32[]{:S(2)}) collective-permute-start(f32[16]{0:T(128)S(1)} %select_reduce_fusion), channel_id=1, source_target_pairs={{0,4},{4,0},{1,5},{5,1},{2,6},{6,2},{3,7},{7,3},{8,12},{12,8},{9,1... | collective-permute-start | bytes 200 | tf_op jit(solution)/shard_map/ppermute | solution.py:18
  411.6 12.8 %collective-permute-done.42 = bf16[128,3584]{1,0:T(8,128)(2,1)S(1)} collective-permute-done((bf16[128,3584]{1,0:T(8,128)(2,1)S(1)}, bf16[128,3584]{1,0:T(8,128)(2,1)S(1)}, u32[]{:S(2)}, u32[]{:S(2)}) %collective-permute-start.42) | collective-permute-done | bytes 917536 | tf_op jit(solution)/shard_map/ppermute | solution.py:38
  424.4 4.5 %collective-permute-start.43 = (bf16[128,3584]{1,0:T(8,128)(2,1)S(1)}, bf16[128,3584]{1,0:T(8,128)(2,1)S(1)}, u32[]{:S(2)}, u32[]{:S(2)}) collective-permute-start(bf16[128,3584]{1,0:T(8,128)(2,1)S(1)} %collective-permute-done.42), channel_id=1, source_target_pairs={{0,4},{4,0},{1,5},{5,1},{2,6},{6,2},{3,7},{7,3},{8,12},{12,8},{9,1... | collective-permute-start | bytes 2752520 | tf_op jit(solution)/shard_map/ppermute | solution.py:18
  (207 shorter events, 177.8 us)
Async XLA Ops:
  12.6 107.4 %collective-permute-start.6 = (bf16[3584,512]{1,0:T(8,128)(2,1)}, bf16[3584,512]{1,0:T(8,128)(2,1)}, u32[]{:S(2)}, u32[]{:S(2)}) collective-permute-start(bf16[3584,512]{1,0:T(8,128)(2,1)} %dynamic-slice_bitcast_fusion.1), channel_id=1, source_target_pairs={{0,4},{4,0},{1,5},{5,1},{2,6},{6,2},{3,7},{7,3},{8,12},{12,8},{9,1... | collective-permute-start | bytes 11010056 | tf_op jit(solution)/shard_map/ppermute | solution.py:18
  15.9 158.4 %collective-permute-start.9 = (bf16[512,3584]{1,0:T(8,128)(2,1)}, bf16[512,3584]{1,0:T(8,128)(2,1)}, u32[]{:S(2)}, u32[]{:S(2)}) collective-permute-start(bf16[512,3584]{1,0:T(8,128)(2,1)} %dynamic-slice_bitcast_fusion), channel_id=1, source_target_pairs={{0,4},{4,0},{1,5},{5,1},{2,6},{6,2},{3,7},{7,3},{8,12},{12,8},{9,1... | collective-permute-start | bytes 11010056 | tf_op jit(solution)/shard_map/ppermute | solution.py:18
  53.2 40.9 %collective-permute-start.21 = (bf16[128,3584]{1,0:T(8,128)(2,1)}, bf16[128,3584]{1,0:T(8,128)(2,1)S(1)}, u32[]{:S(2)}, u32[]{:S(2)}) collective-permute-start(bf16[128,3584]{1,0:T(8,128)(2,1)} %dynamic-slice_bitcast_fusion.2), channel_id=1, source_target_pairs={{0,1},{1,2},{2,3},{4,5},{5,6},{6,7},{8,9},{9,10},{10,11},{12,13},{... | collective-permute-start | bytes 2752520 | tf_op jit(solution)/shard_map/ppermute | solution.py:45
  57.7 40.4 %collective-permute-start.23 = (bf16[128,3584]{1,0:T(8,128)(2,1)}, bf16[128,3584]{1,0:T(8,128)(2,1)S(1)}, u32[]{:S(2)}, u32[]{:S(2)}) collective-permute-start(bf16[128,3584]{1,0:T(8,128)(2,1)} %dynamic-slice_bitcast_fusion.2), channel_id=1, source_target_pairs={{1,0},{2,1},{3,2},{5,4},{6,5},{7,6},{9,8},{10,9},{11,10},{13,12},{... | collective-permute-start | bytes 2752520 | tf_op jit(solution)/shard_map/ppermute | solution.py:46
  59.6 33.7 %collective-permute-start.5 = (bf16[128,3584]{1,0:T(8,128)(2,1)}, bf16[128,3584]{1,0:T(8,128)(2,1)S(1)}, u32[]{:S(2)}, u32[]{:S(2)}) collective-permute-start(bf16[128,3584]{1,0:T(8,128)(2,1)} %collective-permute-done.4), channel_id=1, source_target_pairs={{2,3},{6,7},{10,11},{14,15},{18,19},{22,23},{26,27},{30,31}} | collective-permute-start | bytes 2752520 | tf_op jit(solution)/shard_map/ppermute | solution.py:45
  113.9 54.4 %collective-permute-start.25 = (bf16[128,3584]{1,0:T(8,128)(2,1)S(1)}, bf16[128,3584]{1,0:T(8,128)(2,1)S(1)}, u32[]{:S(2)}, u32[]{:S(2)}) collective-permute-start(bf16[128,3584]{1,0:T(8,128)(2,1)S(1)} %copy-done.9), channel_id=1, source_target_pairs={{0,1},{1,2},{2,3},{4,5},{5,6},{6,7},{8,9},{9,10},{10,11},{12,13},{... | collective-permute-start | bytes 2752520 | tf_op jit(solution)/shard_map/ppermute | solution.py:45
  117.0 55.4 %collective-permute-start.26 = (bf16[128,3584]{1,0:T(8,128)(2,1)S(1)}, bf16[128,3584]{1,0:T(8,128)(2,1)S(1)}, u32[]{:S(2)}, u32[]{:S(2)}) collective-permute-start(bf16[128,3584]{1,0:T(8,128)(2,1)S(1)} %copy-done.9), channel_id=1, source_target_pairs={{1,0},{2,1},{3,2},{5,4},{6,5},{7,6},{9,8},{10,9},{11,10},{13,12},{... | collective-permute-start | bytes 2752520 | tf_op jit(solution)/shard_map/ppermute | solution.py:46
  124.4 30.6 %collective-permute-start.7 = (f32[512,512]{1,0:T(8,128)S(1)}, f32[512,512]{1,0:T(8,128)S(1)}, u32[]{:S(2)}, u32[]{:S(2)}) collective-permute-start(f32[512,512]{1,0:T(8,128)S(1)} %fusion.58), channel_id=1, source_target_pairs={{0,4},{4,0},{1,5},{5,1},{2,6},{6,2},{3,7},{7,3},{8,12},{12,8},{9,1... | collective-permute-start | bytes 3145736 | tf_op jit(solution)/shard_map/ppermute | solution.py:18
  168.1 33.5 %collective-permute-start.34 = (f32[512,512]{1,0:T(8,128)}, f32[512,512]{1,0:T(8,128)}, u32[]{:S(2)}, u32[]{:S(2)}) collective-permute-start(f32[512,512]{1,0:T(8,128)} %fusion.56), channel_id=1, source_target_pairs={{0,4},{4,0},{1,5},{5,1},{2,6},{6,2},{3,7},{7,3},{8,12},{12,8},{9,1... | collective-permute-start | bytes 3145736 | tf_op jit(solution)/shard_map/ppermute | solution.py:18
  180.9 26.9 %collective-permute-start.13 = (bf16[128,3584]{1,0:T(8,128)(2,1)S(1)}, bf16[128,3584]{1,0:T(8,128)(2,1)S(1)}, u32[]{:S(2)}, u32[]{:S(2)}) collective-permute-start(bf16[128,3584]{1,0:T(8,128)(2,1)S(1)} %fusion.28), channel_id=1, source_target_pairs={{0,1},{4,5},{8,9},{12,13},{16,17},{20,21},{24,25},{28,29}} | collective-permute-start | bytes 2752520 | tf_op jit(solution)/shard_map/ppermute | solution.py:58
  199.9 28.6 %collective-permute-start.30 = (bf16[128,3584]{1,0:T(8,128)(2,1)S(1)}, bf16[128,3584]{1,0:T(8,128)(2,1)S(1)}, u32[]{:S(2)}, u32[]{:S(2)}) collective-permute-start(bf16[128,3584]{1,0:T(8,128)(2,1)S(1)} %collective-permute-done.29), channel_id=1, source_target_pairs={{2,3},{6,7},{10,11},{14,15},{18,19},{22,23},{26,27},{30,31}} | collective-permute-start | bytes 2752520 | tf_op jit(solution)/shard_map/ppermute | solution.py:45
  201.6 26.9 %collective-permute-start.28 = (bf16[128,3584]{1,0:T(8,128)(2,1)S(1)}, bf16[128,3584]{1,0:T(8,128)(2,1)S(1)}, u32[]{:S(2)}, u32[]{:S(2)}) collective-permute-start(bf16[128,3584]{1,0:T(8,128)(2,1)S(1)} %collective-permute-done.27), channel_id=1, source_target_pairs={{1,0},{5,4},{9,8},{13,12},{17,16},{21,20},{25,24},{29,28}} | collective-permute-start | bytes 2752520 | tf_op jit(solution)/shard_map/ppermute | solution.py:46
  208.0 41.4 %collective-permute-start.14 = (bf16[128,3584]{1,0:T(8,128)(2,1)S(1)}, bf16[128,3584]{1,0:T(8,128)(2,1)S(1)}, u32[]{:S(2)}, u32[]{:S(2)}) collective-permute-start(bf16[128,3584]{1,0:T(8,128)(2,1)S(1)} %add_convert_fusion.7), channel_id=1, source_target_pairs={{0,1},{1,2},{4,5},{5,6},{8,9},{9,10},{12,13},{13,14},{16,17},{17,1... | collective-permute-start | bytes 2752520 | tf_op jit(solution)/shard_map/ppermute | solution.py:58
  211.7 33.1 %collective-permute-start.48 = (bf16[256,1280]{1,0:T(8,128)(2,1)S(1)}, bf16[256,1280]{1,0:T(8,128)(2,1)}, u32[]{:S(2)}, u32[]{:S(2)}) collective-permute-start(bf16[256,1280]{1,0:T(8,128)(2,1)S(1)} %collective-permute-done.44), channel_id=1, source_target_pairs={{1,2},{2,3},{5,6},{6,7},{9,10},{10,11},{13,14},{14,15},{17,18},{18... | collective-permute-start | bytes 1966088 | tf_op jit(solution)/shard_map/ppermute | solution.py:45
  213.6 33.1 %collective-permute-start.46 = (bf16[256,1280]{1,0:T(8,128)(2,1)S(1)}, bf16[256,1280]{1,0:T(8,128)(2,1)S(1)}, u32[]{:S(2)}, u32[]{:S(2)}) collective-permute-start(bf16[256,1280]{1,0:T(8,128)(2,1)S(1)} %collective-permute-done.45), channel_id=1, source_target_pairs={{1,0},{2,1},{5,4},{6,5},{9,8},{10,9},{13,12},{14,13},{17,16},{18,1... | collective-permute-start | bytes 1966088 | tf_op jit(solution)/shard_map/ppermute | solution.py:46
  249.8 36.8 %collective-permute-start.16 = (bf16[128,3584]{1,0:T(8,128)(2,1)S(1)}, bf16[128,3584]{1,0:T(8,128)(2,1)}, u32[]{:S(2)}, u32[]{:S(2)}) collective-permute-start(bf16[128,3584]{1,0:T(8,128)(2,1)S(1)} %get-tuple-element.17), channel_id=1, source_target_pairs={{3,2},{7,6},{11,10},{15,14},{19,18},{23,22},{27,26},{31,30}} | collective-permute-start | bytes 2752520 | tf_op jit(solution)/shard_map/ppermute | solution.py:59
  251.1 89.7 %collective-permute-start.15 = (bf16[128,3584]{1,0:T(8,128)(2,1)S(1)}, bf16[128,3584]{1,0:T(8,128)(2,1)}, u32[]{:S(2)}, u32[]{:S(2)}) collective-permute-start(bf16[128,3584]{1,0:T(8,128)(2,1)S(1)} %get-tuple-element.16), channel_id=1, source_target_pairs={{0,1},{1,2},{2,3},{4,5},{5,6},{6,7},{8,9},{9,10},{10,11},{12,13},{... | collective-permute-start | bytes 2752520 | tf_op jit(solution)/shard_map/ppermute | solution.py:58
  285.3 32.7 %collective-permute-start.37 = (bf16[128,3584]{1,0:T(8,128)(2,1)S(1)}, bf16[128,3584]{1,0:T(8,128)(2,1)S(1)}, u32[]{:S(2)}, u32[]{:S(2)}) collective-permute-start(bf16[128,3584]{1,0:T(8,128)(2,1)S(1)} %add_convert_fusion.3), channel_id=1, source_target_pairs={{0,1},{1,2},{4,5},{5,6},{8,9},{9,10},{12,13},{13,14},{16,17},{17,1... | collective-permute-start | bytes 2752520 | tf_op jit(solution)/shard_map/ppermute | solution.py:58
  288.1 32.5 %collective-permute-start.17 = (bf16[128,3584]{1,0:T(8,128)(2,1)S(1)}, bf16[128,3584]{1,0:T(8,128)(2,1)S(1)}, u32[]{:S(2)}, u32[]{:S(2)}) collective-permute-start(bf16[128,3584]{1,0:T(8,128)(2,1)S(1)} %add_convert_fusion.5), channel_id=1, source_target_pairs={{2,1},{3,2},{6,5},{7,6},{10,9},{11,10},{14,13},{15,14},{18,17},{19... | collective-permute-start | bytes 2752520 | tf_op jit(solution)/shard_map/ppermute | solution.py:59
  320.9 37.3 %collective-permute-start.18 = (bf16[128,3584]{1,0:T(8,128)(2,1)S(1)}, bf16[128,3584]{1,0:T(8,128)(2,1)S(1)}, u32[]{:S(2)}, u32[]{:S(2)}) collective-permute-start(bf16[128,3584]{1,0:T(8,128)(2,1)S(1)} %add_convert_fusion.4), channel_id=1, source_target_pairs={{1,0},{2,1},{3,2},{5,4},{6,5},{7,6},{9,8},{10,9},{11,10},{13,12},{... | collective-permute-start | bytes 2752520 | tf_op jit(solution)/shard_map/ppermute | solution.py:59
  338.8 39.1 %collective-permute-start.40 = (bf16[128,3584]{1,0:T(8,128)(2,1)S(1)}, bf16[128,3584]{1,0:T(8,128)(2,1)S(1)}, u32[]{:S(2)}, u32[]{:S(2)}) collective-permute-start(bf16[128,3584]{1,0:T(8,128)(2,1)S(1)} %add_convert_fusion.1), channel_id=1, source_target_pairs={{2,1},{3,2},{6,5},{7,6},{10,9},{11,10},{14,13},{15,14},{18,17},{19... | collective-permute-start | bytes 2752520 | tf_op jit(solution)/shard_map/ppermute | solution.py:59
  361.1 39.2 %collective-permute-start.19 = (bf16[128,3584]{1,0:T(8,128)(2,1)}, bf16[128,3584]{1,0:T(8,128)(2,1)}, u32[]{:S(2)}, u32[]{:S(2)}) collective-permute-start(bf16[128,3584]{1,0:T(8,128)(2,1)} %fusion.26), channel_id=1, source_target_pairs={{0,8},{8,16},{16,24},{1,9},{9,17},{17,25},{2,10},{10,18},{18,26},{... | collective-permute-start | bytes 2752520 | tf_op jit(solution)/shard_map/ppermute | solution.py:38
  364.2 36.4 %collective-permute-start.38 = (bf16[128,3584]{1,0:T(8,128)(2,1)}, bf16[128,3584]{1,0:T(8,128)(2,1)}, u32[]{:S(2)}, u32[]{:S(2)}) collective-permute-start(bf16[128,3584]{1,0:T(8,128)(2,1)} %get-tuple-element.14), channel_id=1, source_target_pairs={{0,1},{1,2},{2,3},{4,5},{5,6},{6,7},{8,9},{9,10},{10,11},{12,13},{... | collective-permute-start | bytes 2752520 | tf_op jit(solution)/shard_map/ppermute | solution.py:58
  400.3 28.7 %collective-permute-start.20 = (bf16[128,3584]{1,0:T(8,128)(2,1)}, bf16[128,3584]{1,0:T(8,128)(2,1)S(1)}, u32[]{:S(2)}, u32[]{:S(2)}) collective-permute-start(bf16[128,3584]{1,0:T(8,128)(2,1)} %collective-permute-done.19), channel_id=1, source_target_pairs={{0,4},{4,0},{1,5},{5,1},{2,6},{6,2},{3,7},{7,3},{8,12},{12,8},{9,1... | collective-permute-start | bytes 2752520 | tf_op jit(solution)/shard_map/ppermute | solution.py:18
  (58 other events, 1108.1 us)

commit v2 on v1

--- a/solution.py
+++ b/solution.py
@@ -4,6 +4,7 @@
 from jax.sharding import PartitionSpec as P
 
 HD = 128
+PIECES = 2
 
 clip_limit = 100.0
 logit_scale = 192.0 ** (-0.5)
@@ -45,22 +46,26 @@
         up.append(lax.ppermute(up[-1], "expert", [(j, j + 1) for j in range(step - 1, n - 1)]))
         down.append(lax.ppermute(down[-1], "expert", [(j, j - 1) for j in range(1, n - step + 1)]))
     blocks = [block] + [jnp.where(place >= r, up[r], down[n - r]) for r in range(1, n)]
-    return blocks, (up[min(2, n - 1)], down[min(2, n - 1)])
+    return blocks, (up[min(2, n - 1)], down[min(2, n - 1)]), (up[-1], down[-1])
 
 
-def collect(parts):
+def collect(parts, behind=()):
     n = lax.axis_size("expert")
     up = down = None
     for step in range(1, n):
         first, second = parts[step], parts[n - step]
         if up is not None:
-            first, second = first + up, second + down
-        up = lax.ppermute(first.astype(jnp.bfloat16), "expert", [(j, j + 1) for j in range(0, min(step, n - 1))])
+            first, second = first + up.astype(jnp.float32), second + down.astype(jnp.float32)
+        first, second = first.astype(jnp.bfloat16), second.astype(jnp.bfloat16)
+        if up is None and behind:
+            first, second = lax.optimization_barrier((first, second) + behind)[:2]
+        up = lax.ppermute(first, "expert", [(j, j + 1) for j in range(0, min(step, n - 1))])
         down = lax.ppermute(
-            second.astype(jnp.bfloat16), "expert", [(j, j - 1) for j in range(max(n - step, 1), n)]
+            second, "expert", [(j, j - 1) for j in range(max(n - step, 1), n)]
         )
-        up, down = up.astype(jnp.float32), down.astype(jnp.float32)
-    return parts[0] + up + down
+        if step == 1:
+            mark = (up, down)
+    return parts[0] + up.astype(jnp.float32) + down.astype(jnp.float32), mark
 
 
 def coefficients(routes, gates, place):
@@ -110,22 +115,23 @@
     gates = jnp.stack([fwd_gates[0], bwd_gates[0]])
     latent = jnp.concatenate([query_latent[0, 0], key_latent[0, 0]], axis=1)
 
-    tokens_all, mark = spread(tokens_half, place)
+    tokens_all, mark, last = spread(tokens_half, place)
     up_own = own_half(w_up[0, 0], 0, core)
     up_other = swap(other_half(w_up[0, 0], 0, core))
     down_own = own_half(w_down[0, 0], 1, core)
     down_other = swap(other_half(w_down[0, 0], 1, core))
     coef = coefficients(routes, gates, place)
-    saved_all, mark = spread(after(saved_half, *mark), place)
-    grads_all, mark = spread(after(grads_half, *mark), place)
-    latent_all, mark = spread(after(latent, *mark), place)
+    saved_all, mark, last = spread(after(saved_half, *mark), place)
+    grads_all, mark, last = spread(after(grads_half, *mark), place)
+    latent_all, mark, last = spread(after(latent, *last), place)
 
     rows = jnp.concatenate(tokens_all, axis=0)
     pre_act = times(rows, up_own) + swap(times(rows, up_other))
     hidden = jax.nn.silu(pre_act).astype(jnp.bfloat16)
     out = times(hidden, down_own) + times(swap(hidden), down_other)
     parts = [out[r * tok:(r + 1) * tok] * coef[r][0][:, None] for r in range(n)]
-    section_half = (tokens_half.astype(jnp.float32) + collect(parts)).astype(jnp.bfloat16)
+    total, mark = collect(parts)
+    section_half = (tokens_half.astype(jnp.float32) + total).astype(jnp.bfloat16)
     fwd_half = shifted(section_half, "pipe", 1)
 
     rows = jnp.concatenate(saved_all, axis=0)
@@ -133,10 +139,16 @@
     rows = jnp.concatenate(grads_all, axis=0)
     back = times_transposed(rows, down_own) + swap(times_transposed(rows, down_other))
     pre_grad = (back * silu_grad(pre_act)).astype(jnp.bfloat16)
-    out = times_transposed(pre_grad, up_own) + times_transposed(swap(pre_grad), up_other)
-    parts = [out[r * tok:(r + 1) * tok] * coef[r][1][:, None] for r in range(n)]
-    grad_half = (grads_half.astype(jnp.float32) + collect(parts)).astype(jnp.bfloat16)
-    bwd_half = shifted(grad_half, "pipe", -1)
+    pre_grad_other = swap(pre_grad)
+    bwd_pieces, mark = [], ()
+    width = grads_half.shape[1] // PIECES
+    for k in range(PIECES):
+        cut = slice(k * width, (k + 1) * width)
+        out = times_transposed(pre_grad, up_own[cut]) + times_transposed(pre_grad_other, up_other[cut])
+        parts = [out[r * tok:(r + 1) * tok] * coef[r][1][:, None] for r in range(n)]
+        total, mark = collect(parts, mark)
+        grad_piece = (grads_half[:, cut].astype(jnp.float32) + total).astype(jnp.bfloat16)
+        bwd_pieces.append(shifted(grad_piece, "pipe", -1))
 
     query_proj = query_weight[0]
     key_proj = key_weight[0]
@@ -158,13 +170,13 @@
     query_clipped = (query_proj.astype(jnp.float32) * col_factor[None, :]).astype(jnp.bfloat16)
     key_clipped = (key_proj.astype(jnp.float32) * col_factor[None, :]).astype(jnp.bfloat16)
 
-    def whole(half):
-        theirs = swap(half)
-        first = jnp.where(core == 0, half, theirs)
-        second = jnp.where(core == 0, theirs, half)
-        return jnp.concatenate([first, second], axis=1)
+    def whole(pieces):
+        theirs = [swap(piece) for piece in pieces]
+        first = [jnp.where(core == 0, a, b) for a, b in zip(pieces, theirs)]
+        second = [jnp.where(core == 0, b, a) for a, b in zip(pieces, theirs)]
+        return jnp.concatenate(first + second, axis=1)
 
-    return (whole(fwd_half)[None], whole(bwd_half)[None], query_clipped[None], key_clipped[None])
+    return (whole([fwd_half])[None], whole(bwd_pieces)[None], query_clipped[None], key_clipped[None])
 
 
 def solution(mesh):

time: 436 us -> 442 us (1.014)
  waiting for transfers between devices: 179 us -> 196 us
  matrix products: 63.5 us -> 69 us
  local copies, waits for them, and re-layouts: 15.5 us -> 10.2 us
  other arithmetic: 29.4 us -> 24.1 us
  starting transfers between devices: 144 us -> 139 us
    ppermute x12, waiting for transfers between devices: 88.2 us -> 120 us  [spread(): lax.ppermute(up[-1], 'expert', [(j, j + 1) for j in range(step - 1, n - 1)])]
    ppermute x12 -> x18, waiting for transfers between devices: 56.5 us -> 38.5 us  [the longest x9 30.5 us: collect(): lax.ppermute(second, 'expert', [(j, j - 1) for j in range(max(n - step, 1...]
    ppermute x12, starting transfers between devices: 32.3 us -> 24.1 us  [spread(): lax.ppermute(down[-1], 'expert', [(j, j - 1) for j in range(1, n - step +...]
    ppermute x2 -> x3, waiting for transfers between devices: 12.8 us -> 17.2 us  [shifted(): return lax.ppermute(block, axis, route)]
    dot_general x4 -> x6, matrix products: 16.4 us -> 20.4 us  [times_transposed(): lax.dot_general(rows, weight, (((1,), (1,)), ((), ())), preferred_element...]
    ppermute x12 -> x18, starting transfers between devices: 38.3 us -> 34.9 us  [the longest x9 17.7 us: collect(): lax.ppermute(second, 'expert', [(j, j - 1) for j in range(max(n - step, 1...]
    convert_element_type x12 -> x14, other arithmetic: 11.4 us -> 9.77 us  [the longest x12 7.32 us: collect(): first, second = (first.astype(jnp.bfloat16), second.astype(jnp.bfloat16))]
    ppermute x10 -> x11, starting transfers between devices: 29.9 us -> 30.4 us  [swap(): return lax.ppermute(block, 'dp', [(0, 1), (1, 0)])]
  transfers between devices with their start and end apart: 51 -> 59, of which waited for: 18 -> 20; matrix products, arithmetic and copies ran while one was open for 23% -> 23% of each run, Pallas kernels for 0% -> 0%
where the time goes in v2:
time: 442 us; the launch traced here: 440 us
  waiting for transfers between devices  196 us (44%)
  starting transfers between devices  139 us (31%)
  matrix products  69 us (16%)
  other arithmetic  24.1 us (5%)
  local copies, waits for them, and re-layouts  10.2 us (2%)
    ppermute x12, waiting for transfers between devices, spread(): lax.ppermute(up[-1], 'expert', [(j, j + 1) for j in range(step - 1, n - 1)])  120 us
    ppermute x12, starting transfers between devices, spread(): lax.ppermute(up[-1], 'expert', [(j, j + 1) for j in range(step - 1, n - 1)])  39.5 us
    dot_general x8, matrix products, times(): return jnp.dot(rows, weight, preferred_element_type=jnp.float32)  34 us
    ppermute x9, waiting for transfers between devices, collect(): lax.ppermute(second, 'expert', [(j, j - 1) for j in range(max(n - step, 1...  30.5 us
    ppermute x11, starting transfers between devices, swap(): return lax.ppermute(block, 'dp', [(0, 1), (1, 0)])  30.4 us
    ppermute x12, starting transfers between devices, spread(): lax.ppermute(down[-1], 'expert', [(j, j - 1) for j in range(1, n - step +...  24.1 us
    dot_general x6, matrix products, times_transposed(): lax.dot_general(rows, weight, (((1,), (1,)), ((), ())), preferred_element...  20.4 us
    ppermute x3, waiting for transfers between devices, coefficients(): value = lax.ppermute(value, 'expert', [(j, (j + r) % n) for j in range(n)])  19.4 us
  transfers between devices with their start and end apart: 59, of which 20 were waited for; matrix products, arithmetic and copies ran while one was open for 23% of the time, Pallas kernels for 0%

profile of v2, /device:TPU:19, one launch (start us, length us, event | category | flops | bytes accessed | tf_op | source)
XLA Modules:
  0.0 440.0 jit_solution(9467902397322418052)
XLA Ops:
  33.7 17.0 %collective-permute-done.11 = f32[2,128]{1,0:T(2,128)S(1)} collective-permute-done((f32[2,128]{1,0:T(2,128)S(1)}, f32[2,128]{1,0:T(2,128)S(1)}, u32[]{:S(2)}, u32[]{:S(2)}) %collective-permute-start.11) | collective-permute-done | bytes 1056 | tf_op jit(solution)/shard_map/ppermute | solution.py:78
  53.2 4.3 collective-permute-start.21
  64.2 28.8 %collective-permute-done.5 = bf16[128,3584]{1,0:T(8,128)(2,1)S(1)} collective-permute-done((bf16[128,3584]{1,0:T(8,128)(2,1)}, bf16[128,3584]{1,0:T(8,128)(2,1)S(1)}, u32[]{:S(2)}, u32[]{:S(2)}) %collective-permute-start.5) | collective-permute-done | bytes 917536 | tf_op jit(solution)/shard_map/ppermute | solution.py:46
  101.9 10.7 %collective-permute-done.22 = bf16[128,3584]{1,0:T(8,128)(2,1)S(1)} collective-permute-done((bf16[128,3584]{1,0:T(8,128)(2,1)S(1)}, bf16[128,3584]{1,0:T(8,128)(2,1)S(1)}, u32[]{:S(2)}, u32[]{:S(2)}) %collective-permute-start.22) | collective-permute-done | bytes 917536 | tf_op jit(solution)/shard_map/ppermute | solution.py:46
  119.6 4.4 fusion.66
  124.0 6.4 %collective-permute-start.7 = (f32[512,512]{1,0:T(8,128)S(1)}, f32[512,512]{1,0:T(8,128)S(1)}, u32[]{:S(2)}, u32[]{:S(2)}) collective-permute-start(f32[512,512]{1,0:T(8,128)S(1)} %fusion.66), channel_id=1, source_target_pairs={{0,4},{4,0},{1,5},{5,1},{2,6},{6,2},{3,7},{7,3},{8,12},{12,8},{9,1... | collective-permute-start | bytes 3145736 | tf_op jit(solution)/shard_map/ppermute | solution.py:19
  133.6 20.1 %collective-permute-done.33 = bf16[128,3584]{1,0:T(8,128)(2,1)S(1)} collective-permute-done((bf16[128,3584]{1,0:T(8,128)(2,1)S(1)}, bf16[128,3584]{1,0:T(8,128)(2,1)S(1)}, u32[]{:S(2)}, u32[]{:S(2)}) %collective-permute-start.33) | collective-permute-done | bytes 917536 | tf_op jit(solution)/shard_map/ppermute | solution.py:46
  162.2 5.1 %fusion.64 = f32[512,512]{1,0:T(8,128)} fusion(bf16[3584,512]{1,0:T(8,128)(2,1)} %collective-permute-done.6, bf16[128,3584]{1,0:T(8,128)(2,1)S(1)} %broadcast_select_fusion, bf16[128,3584]{1,0:T(8,128)(2,1)S(1)} %broadcast_select_fusion.3, bf16[128,3584]{1,0:T(8,128)(2,1)S(1)} %broadcast_select_fusion.6, bf16[128,3584]{1,0:T(8,128)(2,1)S(1)} %dynamic-slice_bitcast_fusion.6), kind=kOutput, calls=%fused_computation.114 | convolution fusion | flops 1893728256 | bytes 8388608 | tf_op jit(solution)/shard_map/dot_general | solution.py:84
  180.9 11.2 %collective-permute-done.29 = bf16[128,3584]{1,0:T(8,128)(2,1)S(1)} collective-permute-done((bf16[128,3584]{1,0:T(8,128)(2,1)S(1)}, bf16[128,3584]{1,0:T(8,128)(2,1)S(1)}, u32[]{:S(2)}, u32[]{:S(2)}) %collective-permute-start.29) | collective-permute-done | bytes 917536 | tf_op jit(solution)/shard_map/ppermute | solution.py:46
  197.7 15.8 %collective-permute-done.30 = bf16[128,3584]{1,0:T(8,128)(2,1)S(1)} collective-permute-done((bf16[128,3584]{1,0:T(8,128)(2,1)S(1)}, bf16[128,3584]{1,0:T(8,128)(2,1)S(1)}, u32[]{:S(2)}, u32[]{:S(2)}) %collective-permute-start.30) | collective-permute-done | bytes 917536 | tf_op jit(solution)/shard_map/ppermute | solution.py:46
  220.1 5.4 %fusion.31 = f32[512,512]{1,0:T(8,128)} fusion(f32[512,512]{1,0:T(8,128)} %collective-permute-done.34, bf16[1,1,7168,512]{3,2,1,0:T(8,128)(2,1)} %param.20, s32[]{:T(128)S(6)} %select_n.123, bf16[128,3584]{1,0:T(8,128)(2,1)S(1)} %broadcast_select_fusion, bf16[128,3584]{1,0:T(8,128)(2,1)S(1)} %broadcast_select_fusion.3, ...), kind=kOutput, calls=%fused_computation.56 | convolution fusion | flops 1893990400 | bytes 9437188 | tf_op jit(solution)/shard_map/dot_general | solution.py:84
  239.5 6.5 %collective-permute-done.52 = bf16[256,1280]{1,0:T(8,128)(2,1)S(1)} collective-permute-done((bf16[256,1280]{1,0:T(8,128)(2,1)S(1)}, bf16[256,1280]{1,0:T(8,128)(2,1)S(1)}, u32[]{:S(2)}, u32[]{:S(2)}) %collective-permute-start.52) | collective-permute-done | bytes 655392 | tf_op jit(solution)/shard_map/ppermute | solution.py:46
  256.4 23.3 %collective-permute-done.56 = bf16[256,1280]{1,0:T(8,128)(2,1)S(1)} collective-permute-done((bf16[256,1280]{1,0:T(8,128)(2,1)S(1)}, bf16[256,1280]{1,0:T(8,128)(2,1)S(1)}, u32[]{:S(2)}, u32[]{:S(2)}) %collective-permute-start.56) | collective-permute-done | bytes 655392 | tf_op jit(solution)/shard_map/ppermute | solution.py:46
  294.4 4.6 %convolution_add_fusion.1 = f32[512,1792]{1,0:T(8,128)} fusion(f32[512,1792]{1,0:T(8,128)S(1)} %fusion.17, bf16[512,512]{1,0:T(8,128)(2,1)S(1)} %fusion.40, bf16[1,1,7168,512]{3,2,1,0:T(8,128)(2,1)} %param.20, s32[]{:T(128)S(6)} %add.182), kind=kOutput, calls=%fused_computation.22 | convolution fusion | flops 940441600 | bytes 9699332 | tf_op jit(solution)/shard_map/dot_general | solution.py:88
  301.3 5.0 %convert_bitcast_fusion.1 = bf16[128,16,8,128]{3,2,1,0:T(8,128)(2,1)} fusion(bf16[1,768,2048]{2,1,0:T(8,128)(2,1)S(1)} %copy-done.4, bf16[1024,1280]{1,0:T(8,128)(2,1)S(1)} %pad_maximum_fusion.3), kind=kOutput, calls=%fused_computation.9 | convolution fusion | flops 3223322624 | bytes 8912896 | tf_op jit(solution)/shard_map/dot_general | solution.py:84
  306.3 7.9 %collective-permute-done.37 = bf16[128,1792]{1,0:T(8,128)(2,1)S(1)} collective-permute-done((bf16[128,1792]{1,0:T(8,128)(2,1)S(1)}, bf16[128,1792]{1,0:T(8,128)(2,1)S(1)}, u32[]{:S(2)}, u32[]{:S(2)}) %collective-permute-start.37) | collective-permute-done | bytes 458784 | tf_op jit(solution)/shard_map/ppermute | solution.py:62
  316.0 4.4 convert_bitcast_fusion
  320.4 6.2 %collective-permute-done.39 = bf16[128,1792]{1,0:T(8,128)(2,1)S(1)} collective-permute-done((bf16[128,1792]{1,0:T(8,128)(2,1)S(1)}, bf16[128,1792]{1,0:T(8,128)(2,1)S(1)}, u32[]{:S(2)}, u32[]{:S(2)}) %collective-permute-start.39) | collective-permute-done | bytes 458784 | tf_op jit(solution)/shard_map/ppermute | solution.py:63
  328.7 14.6 %select_reduce_fusion = f32[16]{0:T(128)S(1)} fusion(pred[1024,1024]{1,0:T(8,128)(4,1)} %broadcast_compare_fusion, bf16[128,16,8,128]{3,2,1,0:T(8,128)(2,1)} %convert_bitcast_fusion, bf16[128,16,8,128]{3,2,1,0:T(8,128)(2,1)} %convert_bitcast_fusion.1), kind=kOutput, calls=%fused_computation | convolution fusion | flops 4345298944 | bytes 9437248 | tf_op jit(solution)/shard_map/qhd,khd->hqk/dot_general | solution.py:164
  357.1 5.6 %collective-permute-done.47 = bf16[128,1792]{1,0:T(8,128)(2,1)S(1)} collective-permute-done((bf16[128,1792]{1,0:T(8,128)(2,1)S(1)}, bf16[128,1792]{1,0:T(8,128)(2,1)S(1)}, u32[]{:S(2)}, u32[]{:S(2)}) %collective-permute-start.47) | collective-permute-done | bytes 458784 | tf_op jit(solution)/shard_map/ppermute | solution.py:63
  368.3 14.1 %collective-permute-done.18 = bf16[128,3584]{1,0:T(8,128)(2,1)S(1)} collective-permute-done((bf16[128,3584]{1,0:T(8,128)(2,1)S(1)}, bf16[128,3584]{1,0:T(8,128)(2,1)S(1)}, u32[]{:S(2)}, u32[]{:S(2)}) %collective-permute-start.18) | collective-permute-done | bytes 917536 | tf_op jit(solution)/shard_map/ppermute | solution.py:63
  400.4 6.1 %collective-permute-done.19 = bf16[128,3584]{1,0:T(8,128)(2,1)S(1)} collective-permute-done((bf16[128,3584]{1,0:T(8,128)(2,1)S(1)}, bf16[128,3584]{1,0:T(8,128)(2,1)S(1)}, u32[]{:S(2)}, u32[]{:S(2)}) %collective-permute-start.19) | collective-permute-done | bytes 917536 | tf_op jit(solution)/shard_map/ppermute | solution.py:39
  417.3 6.8 %collective-permute-done.50 = bf16[128,1792]{1,0:T(8,128)(2,1)S(1)} collective-permute-done((bf16[128,1792]{1,0:T(8,128)(2,1)S(1)}, bf16[128,1792]{1,0:T(8,128)(2,1)S(1)}, u32[]{:S(2)}, u32[]{:S(2)}) %collective-permute-start.50) | collective-permute-done | bytes 458784 | tf_op jit(solution)/shard_map/ppermute | solution.py:39
  424.1 5.5 %collective-permute-start.51 = (bf16[128,1792]{1,0:T(8,128)(2,1)S(1)}, bf16[128,1792]{1,0:T(8,128)(2,1)S(1)}, u32[]{:S(2)}, u32[]{:S(2)}) collective-permute-start(bf16[128,1792]{1,0:T(8,128)(2,1)S(1)} %collective-permute-done.50), channel_id=1, source_target_pairs={{0,4},{4,0},{1,5},{5,1},{2,6},{6,2},{3,7},{7,3},{8,12},{12,8},{9,1... | collective-permute-start | bytes 1376264 | tf_op jit(solution)/shard_map/ppermute | solution.py:19
  (210 shorter events, 198.6 us)
Async XLA Ops:
  12.6 107.0 %collective-permute-start.6 = (bf16[3584,512]{1,0:T(8,128)(2,1)}, bf16[3584,512]{1,0:T(8,128)(2,1)}, u32[]{:S(2)}, u32[]{:S(2)}) collective-permute-start(bf16[3584,512]{1,0:T(8,128)(2,1)} %dynamic-slice_bitcast_fusion.1), channel_id=1, source_target_pairs={{0,4},{4,0},{1,5},{5,1},{2,6},{6,2},{3,7},{7,3},{8,12},{12,8},{9,1... | collective-permute-start | bytes 11010056 | tf_op jit(solution)/shard_map/ppermute | solution.py:19
  15.9 157.7 %collective-permute-start.9 = (bf16[512,3584]{1,0:T(8,128)(2,1)}, bf16[512,3584]{1,0:T(8,128)(2,1)}, u32[]{:S(2)}, u32[]{:S(2)}) collective-permute-start(bf16[512,3584]{1,0:T(8,128)(2,1)} %dynamic-slice_bitcast_fusion), channel_id=1, source_target_pairs={{0,4},{4,0},{1,5},{5,1},{2,6},{6,2},{3,7},{7,3},{8,12},{12,8},{9,1... | collective-permute-start | bytes 11010056 | tf_op jit(solution)/shard_map/ppermute | solution.py:19
  26.4 26.8 %collective-permute-start.4 = (bf16[128,3584]{1,0:T(8,128)(2,1)}, bf16[128,3584]{1,0:T(8,128)(2,1)}, u32[]{:S(2)}, u32[]{:S(2)}) collective-permute-start(bf16[128,3584]{1,0:T(8,128)(2,1)} %collective-permute-done), channel_id=1, source_target_pairs={{1,2},{2,3},{5,6},{6,7},{9,10},{10,11},{13,14},{14,15},{17,18},{18... | collective-permute-start | bytes 2752520 | tf_op jit(solution)/shard_map/ppermute | solution.py:46
  53.2 40.5 %collective-permute-start.21 = (bf16[128,3584]{1,0:T(8,128)(2,1)S(1)}, bf16[128,3584]{1,0:T(8,128)(2,1)S(1)}, u32[]{:S(2)}, u32[]{:S(2)}) collective-permute-start(bf16[128,3584]{1,0:T(8,128)(2,1)S(1)} %dynamic-slice_bitcast_fusion.6), channel_id=1, source_target_pairs={{0,1},{1,2},{2,3},{4,5},{5,6},{6,7},{8,9},{9,10},{10,11},{12,13},{... | collective-permute-start | bytes 2752520 | tf_op jit(solution)/shard_map/ppermute | solution.py:46
  57.5 40.2 %collective-permute-start.23 = (bf16[128,3584]{1,0:T(8,128)(2,1)S(1)}, bf16[128,3584]{1,0:T(8,128)(2,1)S(1)}, u32[]{:S(2)}, u32[]{:S(2)}) collective-permute-start(bf16[128,3584]{1,0:T(8,128)(2,1)S(1)} %dynamic-slice_bitcast_fusion.6), channel_id=1, source_target_pairs={{1,0},{2,1},{3,2},{5,4},{6,5},{7,6},{9,8},{10,9},{11,10},{13,12},{... | collective-permute-start | bytes 2752520 | tf_op jit(solution)/shard_map/ppermute | solution.py:47
  59.4 33.5 %collective-permute-start.5 = (bf16[128,3584]{1,0:T(8,128)(2,1)}, bf16[128,3584]{1,0:T(8,128)(2,1)S(1)}, u32[]{:S(2)}, u32[]{:S(2)}) collective-permute-start(bf16[128,3584]{1,0:T(8,128)(2,1)} %collective-permute-done.4), channel_id=1, source_target_pairs={{2,3},{6,7},{10,11},{14,15},{18,19},{22,23},{26,27},{30,31}} | collective-permute-start | bytes 2752520 | tf_op jit(solution)/shard_map/ppermute | solution.py:46
  113.6 53.9 %collective-permute-start.25 = (bf16[128,3584]{1,0:T(8,128)(2,1)S(1)}, bf16[128,3584]{1,0:T(8,128)(2,1)S(1)}, u32[]{:S(2)}, u32[]{:S(2)}) collective-permute-start(bf16[128,3584]{1,0:T(8,128)(2,1)S(1)} %dynamic-slice_bitcast_fusion.7), channel_id=1, source_target_pairs={{0,1},{1,2},{2,3},{4,5},{5,6},{6,7},{8,9},{9,10},{10,11},{12,13},{... | collective-permute-start | bytes 2752520 | tf_op jit(solution)/shard_map/ppermute | solution.py:46
  116.6 55.0 %collective-permute-start.26 = (bf16[128,3584]{1,0:T(8,128)(2,1)S(1)}, bf16[128,3584]{1,0:T(8,128)(2,1)S(1)}, u32[]{:S(2)}, u32[]{:S(2)}) collective-permute-start(bf16[128,3584]{1,0:T(8,128)(2,1)S(1)} %dynamic-slice_bitcast_fusion.7), channel_id=1, source_target_pairs={{1,0},{2,1},{3,2},{5,4},{6,5},{7,6},{9,8},{10,9},{11,10},{13,12},{... | collective-permute-start | bytes 2752520 | tf_op jit(solution)/shard_map/ppermute | solution.py:47
  124.0 30.6 %collective-permute-start.7 = (f32[512,512]{1,0:T(8,128)S(1)}, f32[512,512]{1,0:T(8,128)S(1)}, u32[]{:S(2)}, u32[]{:S(2)}) collective-permute-start(f32[512,512]{1,0:T(8,128)S(1)} %fusion.66), channel_id=1, source_target_pairs={{0,4},{4,0},{1,5},{5,1},{2,6},{6,2},{3,7},{7,3},{8,12},{12,8},{9,1... | collective-permute-start | bytes 3145736 | tf_op jit(solution)/shard_map/ppermute | solution.py:19
  167.3 52.8 %collective-permute-start.34 = (f32[512,512]{1,0:T(8,128)}, f32[512,512]{1,0:T(8,128)}, u32[]{:S(2)}, u32[]{:S(2)}) collective-permute-start(f32[512,512]{1,0:T(8,128)} %fusion.64), channel_id=1, source_target_pairs={{0,4},{4,0},{1,5},{5,1},{2,6},{6,2},{3,7},{7,3},{8,12},{12,8},{9,1... | collective-permute-start | bytes 3145736 | tf_op jit(solution)/shard_map/ppermute | solution.py:19
  167.4 24.6 %collective-permute-start.29 = (bf16[128,3584]{1,0:T(8,128)(2,1)S(1)}, bf16[128,3584]{1,0:T(8,128)(2,1)S(1)}, u32[]{:S(2)}, u32[]{:S(2)}) collective-permute-start(bf16[128,3584]{1,0:T(8,128)(2,1)S(1)} %collective-permute-done.25), channel_id=1, source_target_pairs={{1,2},{2,3},{5,6},{6,7},{9,10},{10,11},{13,14},{14,15},{17,18},{18... | collective-permute-start | bytes 2752520 | tf_op jit(solution)/shard_map/ppermute | solution.py:46
  196.4 36.5 %collective-permute-start.14 = (bf16[128,3584]{1,0:T(8,128)(2,1)S(1)}, bf16[128,3584]{1,0:T(8,128)(2,1)S(1)}, u32[]{:S(2)}, u32[]{:S(2)}) collective-permute-start(bf16[128,3584]{1,0:T(8,128)(2,1)S(1)} %add_convert_fusion.3), channel_id=1, source_target_pairs={{0,1},{1,2},{4,5},{5,6},{8,9},{9,10},{12,13},{13,14},{16,17},{17,1... | collective-permute-start | bytes 2752520 | tf_op jit(solution)/shard_map/ppermute | solution.py:62
  217.9 33.5 %collective-permute-start.31 = (f32[512,512]{1,0:T(8,128)S(1)}, f32[512,512]{1,0:T(8,128)}, u32[]{:S(2)}, u32[]{:S(2)}) collective-permute-start(f32[512,512]{1,0:T(8,128)S(1)} %fusion.65), channel_id=1, source_target_pairs={{0,4},{4,0},{1,5},{5,1},{2,6},{6,2},{3,7},{7,3},{8,12},{12,8},{9,1... | collective-permute-start | bytes 3145736 | tf_op jit(solution)/shard_map/ppermute | solution.py:19
  234.2 48.3 %collective-permute-start.16 = (bf16[128,3584]{1,0:T(8,128)(2,1)S(1)}, bf16[128,3584]{1,0:T(8,128)(2,1)S(1)}, u32[]{:S(2)}, u32[]{:S(2)}) collective-permute-start(bf16[128,3584]{1,0:T(8,128)(2,1)S(1)} %get-tuple-element.19), channel_id=1, source_target_pairs={{3,2},{7,6},{11,10},{15,14},{19,18},{23,22},{27,26},{31,30}} | collective-permute-start | bytes 2752520 | tf_op jit(solution)/shard_map/ppermute | solution.py:63
  235.4 132.8 %collective-permute-start.15 = (bf16[128,3584]{1,0:T(8,128)(2,1)}, bf16[128,3584]{1,0:T(8,128)(2,1)}, u32[]{:S(2)}, u32[]{:S(2)}) collective-permute-start(bf16[128,3584]{1,0:T(8,128)(2,1)} %get-tuple-element.18), channel_id=1, source_target_pairs={{0,1},{1,2},{2,3},{4,5},{5,6},{6,7},{8,9},{9,10},{10,11},{12,13},{... | collective-permute-start | bytes 2752520 | tf_op jit(solution)/shard_map/ppermute | solution.py:62
  246.0 33.7 %collective-permute-start.56 = (bf16[256,1280]{1,0:T(8,128)(2,1)S(1)}, bf16[256,1280]{1,0:T(8,128)(2,1)S(1)}, u32[]{:S(2)}, u32[]{:S(2)}) collective-permute-start(bf16[256,1280]{1,0:T(8,128)(2,1)S(1)} %collective-permute-done.52), channel_id=1, source_target_pairs={{1,2},{2,3},{5,6},{6,7},{9,10},{10,11},{13,14},{14,15},{17,18},{18... | collective-permute-start | bytes 1966088 | tf_op jit(solution)/shard_map/ppermute | solution.py:46
  248.0 33.7 %collective-permute-start.54 = (bf16[256,1280]{1,0:T(8,128)(2,1)S(1)}, bf16[256,1280]{1,0:T(8,128)(2,1)S(1)}, u32[]{:S(2)}, u32[]{:S(2)}) collective-permute-start(bf16[256,1280]{1,0:T(8,128)(2,1)S(1)} %collective-permute-done.53), channel_id=1, source_target_pairs={{1,0},{2,1},{5,4},{6,5},{9,8},{10,9},{13,12},{14,13},{17,16},{18,1... | collective-permute-start | bytes 1966088 | tf_op jit(solution)/shard_map/ppermute | solution.py:47
  255.0 30.6 %collective-permute-start.35 = (bf16[512,512]{1,0:T(8,128)(2,1)S(1)}, bf16[512,512]{1,0:T(8,128)(2,1)S(1)}, u32[]{:S(2)}, u32[]{:S(2)}) collective-permute-start(bf16[512,512]{1,0:T(8,128)(2,1)S(1)} %fusion.40), channel_id=1, source_target_pairs={{0,4},{4,0},{1,5},{5,1},{2,6},{6,2},{3,7},{7,3},{8,12},{12,8},{9,1... | collective-permute-start | bytes 1572872 | tf_op jit(solution)/shard_map/ppermute | solution.py:19
  283.7 66.5 %collective-permute-start.17 = (bf16[128,3584]{1,0:T(8,128)(2,1)}, bf16[128,3584]{1,0:T(8,128)(2,1)}, u32[]{:S(2)}, u32[]{:S(2)}) collective-permute-start(bf16[128,3584]{1,0:T(8,128)(2,1)} %add_convert_fusion.1), channel_id=1, source_target_pairs={{2,1},{3,2},{6,5},{7,6},{10,9},{11,10},{14,13},{15,14},{18,17},{19... | collective-permute-start | bytes 2752520 | tf_op jit(solution)/shard_map/ppermute | solution.py:63
  351.6 30.7 %collective-permute-start.18 = (bf16[128,3584]{1,0:T(8,128)(2,1)S(1)}, bf16[128,3584]{1,0:T(8,128)(2,1)S(1)}, u32[]{:S(2)}, u32[]{:S(2)}) collective-permute-start(bf16[128,3584]{1,0:T(8,128)(2,1)S(1)} %add_convert_fusion), channel_id=1, source_target_pairs={{1,0},{2,1},{3,2},{5,4},{6,5},{7,6},{9,8},{10,9},{11,10},{13,12},{... | collective-permute-start | bytes 2752520 | tf_op jit(solution)/shard_map/ppermute | solution.py:63
  353.6 55.3 %collective-permute-start.38 = (bf16[128,1792]{1,0:T(8,128)(2,1)S(1)}, bf16[128,1792]{1,0:T(8,128)(2,1)S(1)}, u32[]{:S(2)}, u32[]{:S(2)}) collective-permute-start(bf16[128,1792]{1,0:T(8,128)(2,1)S(1)} %get-tuple-element.20), channel_id=1, source_target_pairs={{0,1},{1,2},{2,3},{4,5},{5,6},{6,7},{8,9},{9,10},{10,11},{12,13},{... | collective-permute-start | bytes 1376264 | tf_op jit(solution)/shard_map/ppermute | solution.py:62
  363.0 26.4 %collective-permute-start.45 = (bf16[128,1792]{1,0:T(8,128)(2,1)S(1)}, bf16[128,1792]{1,0:T(8,128)(2,1)S(1)}, u32[]{:S(2)}, u32[]{:S(2)}) collective-permute-start(bf16[128,1792]{1,0:T(8,128)(2,1)S(1)} %get-tuple-element.22), channel_id=1, source_target_pairs={{0,1},{1,2},{4,5},{5,6},{8,9},{9,10},{12,13},{13,14},{16,17},{17,1... | collective-permute-start | bytes 1376264 | tf_op jit(solution)/shard_map/ppermute | solution.py:62
  364.3 27.9 %collective-permute-start.48 = (bf16[128,1792]{1,0:T(8,128)(2,1)S(1)}, bf16[128,1792]{1,0:T(8,128)(2,1)S(1)}, u32[]{:S(2)}, u32[]{:S(2)}) collective-permute-start(bf16[128,1792]{1,0:T(8,128)(2,1)S(1)} %get-tuple-element.23), channel_id=1, source_target_pairs={{2,1},{3,2},{6,5},{7,6},{10,9},{11,10},{14,13},{15,14},{18,17},{19... | collective-permute-start | bytes 1376264 | tf_op jit(solution)/shard_map/ppermute | solution.py:63
  406.5 30.4 %collective-permute-start.20 = (bf16[128,3584]{1,0:T(8,128)(2,1)S(1)}, bf16[128,3584]{1,0:T(8,128)(2,1)S(1)}, u32[]{:S(2)}, u32[]{:S(2)}) collective-permute-start(bf16[128,3584]{1,0:T(8,128)(2,1)S(1)} %collective-permute-done.19), channel_id=1, source_target_pairs={{0,4},{4,0},{1,5},{5,1},{2,6},{6,2},{3,7},{7,3},{8,12},{12,8},{9,1... | collective-permute-start | bytes 2752520 | tf_op jit(solution)/shard_map/ppermute | solution.py:19
  (57 other events, 1068.2 us)

commit v3 on v2

--- a/solution.py
+++ b/solution.py
@@ -4,7 +4,8 @@
 from jax.sharding import PartitionSpec as P
 
 HD = 128
-PIECES = 2
+PIECES = 1
+LANES = 128
 
 clip_limit = 100.0
 logit_scale = 192.0 ** (-0.5)
@@ -39,14 +40,19 @@
     return lax.ppermute(block, axis, route)
 
 
-def spread(block, place):
+def spread(block, place, beside=()):
     n = lax.axis_size("expert")
     up, down = [block], [block]
     for step in range(1, n):
-        up.append(lax.ppermute(up[-1], "expert", [(j, j + 1) for j in range(step - 1, n - 1)]))
-        down.append(lax.ppermute(down[-1], "expert", [(j, j - 1) for j in range(1, n - step + 1)]))
+        higher, lower = up[-1], down[-1]
+        if step > 1:
+            extra = tuple(beside) if step == 2 else ()
+            higher, lower = lax.optimization_barrier((higher, lower) + extra)[:2]
+        up.append(lax.ppermute(higher, "expert", [(j, j + 1) for j in range(step - 1, n - 1)]))
+        down.append(lax.ppermute(lower, "expert", [(j, j - 1) for j in range(1, n - step + 1)]))
     blocks = [block] + [jnp.where(place >= r, up[r], down[n - r]) for r in range(1, n)]
-    return blocks, (up[min(2, n - 1)], down[min(2, n - 1)]), (up[-1], down[-1])
+    marks = [(up[min(s, n - 1)], down[min(s, n - 1)]) for s in (1, 2)]
+    return blocks, marks
 
 
 def collect(parts, behind=()):
@@ -57,8 +63,8 @@
         if up is not None:
             first, second = first + up.astype(jnp.float32), second + down.astype(jnp.float32)
         first, second = first.astype(jnp.bfloat16), second.astype(jnp.bfloat16)
-        if up is None and behind:
-            first, second = lax.optimization_barrier((first, second) + behind)[:2]
+        extra = behind if up is None else ()
+        first, second = lax.optimization_barrier((first, second) + extra)[:2]
         up = lax.ppermute(first, "expert", [(j, j + 1) for j in range(0, min(step, n - 1))])
         down = lax.ppermute(
             second, "expert", [(j, j - 1) for j in range(max(n - step, 1), n)]
@@ -68,16 +74,15 @@
     return parts[0] + up.astype(jnp.float32) + down.astype(jnp.float32), mark
 
 
-def coefficients(routes, gates, place):
-    n = lax.axis_size("expert")
-    result = []
-    for r in range(n):
-        target = lax.rem(place + r, n)
-        value = jnp.sum(jnp.where(routes == target, gates, 0.0), axis=-1)
-        if r:
-            value = lax.ppermute(value, "expert", [(j, (j + r) % n) for j in range(n)])
-        result.append(value)
-    return result
+def gate_columns(routes, gates):
+    experts = jnp.arange(LANES // 2, dtype=jnp.int32)
+    hit = routes[:, :, None] == experts[None, None, :]
+    return jnp.sum(jnp.where(hit, gates[:, :, None], 0.0), axis=1)
+
+
+def column_of(block, index):
+    lanes = jnp.arange(block.shape[1], dtype=jnp.int32)
+    return jnp.sum(jnp.where(lanes[None, :] == index, block.astype(jnp.float32), 0.0), axis=1)
 
 
 def times(rows, weight):
@@ -111,19 +116,26 @@
     tokens_half = own_half(fwd_tokens[0], 1, core)
     saved_half = own_half(bwd_saved[0], 1, core)
     grads_half = own_half(bwd_grads[0], 1, core)
-    routes = jnp.stack([fwd_routes[0], bwd_routes[0]])
-    gates = jnp.stack([fwd_gates[0], bwd_gates[0]])
+    weighing = jnp.concatenate(
+        [gate_columns(fwd_routes[0], fwd_gates[0]), gate_columns(bwd_routes[0], bwd_gates[0])], axis=1
+    ).astype(jnp.bfloat16)
     latent = jnp.concatenate([query_latent[0, 0], key_latent[0, 0]], axis=1)
 
-    tokens_all, mark, last = spread(tokens_half, place)
+    width_half = tokens_half.shape[1]
     up_own = own_half(w_up[0, 0], 0, core)
     up_other = swap(other_half(w_up[0, 0], 0, core))
     down_own = own_half(w_down[0, 0], 1, core)
     down_other = swap(other_half(w_down[0, 0], 1, core))
-    coef = coefficients(routes, gates, place)
-    saved_all, mark, last = spread(after(saved_half, *mark), place)
-    grads_all, mark, last = spread(after(grads_half, *mark), place)
-    latent_all, mark, last = spread(after(latent, *last), place)
+    packed = jnp.concatenate([tokens_half, weighing], axis=1)
+    packed_all, marks = spread(packed, place, (up_other, down_other))
+    tokens_all = [block[:, :width_half] for block in packed_all]
+    coef = [
+        (column_of(block[:, width_half:], place), column_of(block[:, width_half:], place + LANES // 2))
+        for block in packed_all
+    ]
+    saved_all, marks = spread(after(saved_half, *marks[1]), place)
+    latent_all, marks = spread(after(latent, *marks[1]), place)
+    grads_all, unused = spread(after(grads_half, *marks[1]), place, latent_all)
 
     rows = jnp.concatenate(tokens_all, axis=0)
     pre_act = times(rows, up_own) + swap(times(rows, up_other))
@@ -146,7 +158,7 @@
         cut = slice(k * width, (k + 1) * width)
         out = times_transposed(pre_grad, up_own[cut]) + times_transposed(pre_grad_other, up_other[cut])
         parts = [out[r * tok:(r + 1) * tok] * coef[r][1][:, None] for r in range(n)]
-        total, mark = collect(parts, mark)
+        total, mark = collect(parts, mark or (section_half,))
         grad_piece = (grads_half[:, cut].astype(jnp.float32) + total).astype(jnp.bfloat16)
         bwd_pieces.append(shifted(grad_piece, "pipe", -1))
 

time: 442 us -> 443 us (level)
  waiting for transfers between devices: 196 us -> 217 us
  starting transfers between devices: 139 us -> 122 us
  matrix products: 69 us -> 58.5 us
  other arithmetic: 24.1 us -> 32 us
    ppermute x27 -> x24, waiting for transfers between devices: 141 us -> 160 us  [the longest x12 152 us: spread(): lax.ppermute(higher, 'expert', [(j, j + 1) for j in range(step - 1, n - 1)])]
    ppermute x11 -> x10, starting transfers between devices: 30.4 us -> 18 us  [swap(): return lax.ppermute(block, 'dp', [(0, 1), (1, 0)])]
    ppermute x27 -> x24, starting transfers between devices: 65.9 us -> 72.7 us  [the longest x12 42.8 us: spread(): lax.ppermute(lower, 'expert', [(j, j - 1) for j in range(1, n - step + 1)])]
    ppermute x9 -> x6, waiting for transfers between devices: 30.5 us -> 36.4 us  [collect(): lax.ppermute(second, 'expert', [(j, j - 1) for j in range(max(n - step, 1...]
    dot_general x8, matrix products: 34 us -> 28.2 us  [times(): return jnp.dot(rows, weight, preferred_element_type=jnp.float32)]
    ppermute x9 -> x6, starting transfers between devices: 17.2 us -> 12.2 us  [collect(): lax.ppermute(first, 'expert', [(j, j + 1) for j in range(0, min(step, n -...]
    ppermute x9 -> x6, starting transfers between devices: 17.7 us -> 13.6 us  [collect(): lax.ppermute(second, 'expert', [(j, j - 1) for j in range(max(n - step, 1...]
    ppermute x3 -> x2, waiting for transfers between devices: 17.2 us -> 13.5 us  [shifted(): return lax.ppermute(block, axis, route)]
  transfers between devices with their start and end apart: 59 -> 48, of which waited for: 20 -> 22; matrix products, arithmetic and copies ran while one was open for 23% -> 20% of each run, Pallas kernels for 0% -> 0%
where the time goes in v3:
time: 443 us; the launch traced here: 441 us
  waiting for transfers between devices  217 us (49%)
  starting transfers between devices  122 us (28%)
  matrix products  58.5 us (13%)
  other arithmetic  32 us (7%)
  local copies, waits for them, and re-layouts  10.1 us (2%)
    ppermute x12, waiting for transfers between devices, spread(): lax.ppermute(higher, 'expert', [(j, j + 1) for j in range(step - 1, n - 1)])  152 us
    ppermute x12, starting transfers between devices, spread(): lax.ppermute(lower, 'expert', [(j, j - 1) for j in range(1, n - step + 1)])  42.8 us
    ppermute x6, waiting for transfers between devices, collect(): lax.ppermute(second, 'expert', [(j, j - 1) for j in range(max(n - step, 1...  36.4 us
    ppermute x12, starting transfers between devices, spread(): lax.ppermute(higher, 'expert', [(j, j + 1) for j in range(step - 1, n - 1)])  29.9 us
    dot_general x8, matrix products, times(): return jnp.dot(rows, weight, preferred_element_type=jnp.float32)  28.2 us
    ppermute x10, starting transfers between devices, swap(): return lax.ppermute(block, 'dp', [(0, 1), (1, 0)])  18 us
    dot_general x4, matrix products, times_transposed(): lax.dot_general(rows, weight, (((1,), (1,)), ((), ())), preferred_element...  17.2 us
    ppermute x6, starting transfers between devices, collect(): lax.ppermute(second, 'expert', [(j, j - 1) for j in range(max(n - step, 1...  13.6 us
  transfers between devices with their start and end apart: 48, of which 22 were waited for; matrix products, arithmetic and copies ran while one was open for 20% of the time, Pallas kernels for 0%

profile of v3, /device:TPU:19, one launch (start us, length us, event | category | flops | bytes accessed | tf_op | source)
XLA Modules:
  0.0 441.2 jit_solution(16345990223731033540)
XLA Ops:
  0.7 4.3 dynamic-slice_bitcast_fusion.1
  17.0 19.6 %collective-permute-done = bf16[128,3712]{1,0:T(8,128)(2,1)} collective-permute-done((bf16[128,3712]{1,0:T(8,128)(2,1)}, bf16[128,3712]{1,0:T(8,128)(2,1)}, u32[]{:S(2)}, u32[]{:S(2)}) %collective-permute-start) | collective-permute-done | bytes 950304 | tf_op jit(solution)/shard_map/ppermute | solution.py:51
  41.4 5.3 %collective-permute-start.5 = (bf16[128,3712]{1,0:T(8,128)(2,1)}, bf16[128,3712]{1,0:T(8,128)(2,1)}, u32[]{:S(2)}, u32[]{:S(2)}) collective-permute-start(bf16[128,3712]{1,0:T(8,128)(2,1)} %collective-permute-done.1), channel_id=1, source_target_pairs={{1,0},{2,1},{5,4},{6,5},{9,8},{10,9},{13,12},{14,13},{17,16},{18,1... | collective-permute-start | bytes 2850824 | tf_op jit(solution)/shard_map/ppermute | solution.py:52
  46.8 16.4 %collective-permute-done.4 = bf16[128,3712]{1,0:T(8,128)(2,1)} collective-permute-done((bf16[128,3712]{1,0:T(8,128)(2,1)}, bf16[128,3712]{1,0:T(8,128)(2,1)}, u32[]{:S(2)}, u32[]{:S(2)}) %collective-permute-start.4) | collective-permute-done | bytes 950304 | tf_op jit(solution)/shard_map/ppermute | solution.py:51
  74.5 30.5 %collective-permute-done.7 = bf16[128,3712]{1,0:T(8,128)(2,1)S(1)} collective-permute-done((bf16[128,3712]{1,0:T(8,128)(2,1)}, bf16[128,3712]{1,0:T(8,128)(2,1)S(1)}, u32[]{:S(2)}, u32[]{:S(2)}) %collective-permute-start.7) | collective-permute-done | bytes 950304 | tf_op jit(solution)/shard_map/ppermute | solution.py:51
  107.8 4.2 fusion.58
  117.9 6.5 %collective-permute-start.21 = (bf16[128,3584]{1,0:T(8,128)(2,1)S(1)}, bf16[128,3584]{1,0:T(8,128)(2,1)}, u32[]{:S(2)}, u32[]{:S(2)}) collective-permute-start(bf16[128,3584]{1,0:T(8,128)(2,1)S(1)} %collective-permute-done.19), channel_id=1, source_target_pairs={{1,0},{2,1},{5,4},{6,5},{9,8},{10,9},{13,12},{14,13},{17,16},{18,1... | collective-permute-start | bytes 2752520 | tf_op jit(solution)/shard_map/ppermute | solution.py:52
  124.9 16.6 %collective-permute-done.20 = bf16[128,3584]{1,0:T(8,128)(2,1)} collective-permute-done((bf16[128,3584]{1,0:T(8,128)(2,1)S(1)}, bf16[128,3584]{1,0:T(8,128)(2,1)}, u32[]{:S(2)}, u32[]{:S(2)}) %collective-permute-start.20) | collective-permute-done | bytes 917536 | tf_op jit(solution)/shard_map/ppermute | solution.py:51
  145.2 4.2 collective-permute-start.23
  179.5 12.9 %collective-permute-done.24 = bf16[256,1280]{1,0:T(8,128)(2,1)S(1)} collective-permute-done((bf16[256,1280]{1,0:T(8,128)(2,1)S(1)}, bf16[256,1280]{1,0:T(8,128)(2,1)S(1)}, u32[]{:S(2)}, u32[]{:S(2)}) %collective-permute-start.24) | collective-permute-done | bytes 655392 | tf_op jit(solution)/shard_map/ppermute | solution.py:51
  193.1 5.1 %fusion.56 = f32[512,512]{1,0:T(8,128)} fusion(bf16[3584,512]{1,0:T(8,128)(2,1)} %collective-permute-done.2, bf16[128,3584]{1,0:T(8,128)(2,1)S(1)} %broadcast_select_fusion.3, bf16[128,3584]{1,0:T(8,128)(2,1)S(1)} %broadcast_select_fusion.5, bf16[128,3584]{1,0:T(8,128)(2,1)S(1)} %broadcast_select_fusion.7, bf16[128,3584]{1,0:T(8,128)(2,1)S(1)} %dynamic-slice_bitcast_fusion.2), kind=kOutput, calls=%fused_computation.97 | convolution fusion | flops 1893728256 | bytes 8388608 | tf_op jit(solution)/shard_map/dot_general | solution.py:89
  203.8 11.9 %collective-permute-start.27 = (bf16[128,3584]{1,0:T(8,128)(2,1)S(1)}, bf16[128,3584]{1,0:T(8,128)(2,1)S(1)}, u32[]{:S(2)}, u32[]{:S(2)}) collective-permute-start(bf16[128,3584]{1,0:T(8,128)(2,1)S(1)} %dynamic-slice_bitcast_fusion.3), channel_id=1, source_target_pairs={{1,0},{2,1},{3,2},{5,4},{6,5},{7,6},{9,8},{10,9},{11,10},{13,12},{... | collective-permute-start | bytes 2752520 | tf_op jit(solution)/shard_map/ppermute | solution.py:52
  215.8 18.8 %collective-permute-done.29 = bf16[256,1280]{1,0:T(8,128)(2,1)S(1)} collective-permute-done((bf16[256,1280]{1,0:T(8,128)(2,1)S(1)}, bf16[256,1280]{1,0:T(8,128)(2,1)S(1)}, u32[]{:S(2)}, u32[]{:S(2)}) %collective-permute-start.29) | collective-permute-done | bytes 655392 | tf_op jit(solution)/shard_map/ppermute | solution.py:51
  247.4 13.6 %collective-permute-done.30 = bf16[128,3584]{1,0:T(8,128)(2,1)S(1)} collective-permute-done((bf16[128,3584]{1,0:T(8,128)(2,1)S(1)}, bf16[128,3584]{1,0:T(8,128)(2,1)S(1)}, u32[]{:S(2)}, u32[]{:S(2)}) %collective-permute-start.30) | collective-permute-done | bytes 917536 | tf_op jit(solution)/shard_map/ppermute | solution.py:51
  265.9 18.0 %collective-permute-done.33 = bf16[128,3584]{1,0:T(8,128)(2,1)S(1)} collective-permute-done((bf16[128,3584]{1,0:T(8,128)(2,1)S(1)}, bf16[128,3584]{1,0:T(8,128)(2,1)S(1)}, u32[]{:S(2)}, u32[]{:S(2)}) %collective-permute-start.33) | collective-permute-done | bytes 917536 | tf_op jit(solution)/shard_map/ppermute | solution.py:51
  285.0 6.2 %fusion.57 = f32[512,512]{1,0:T(8,128)} fusion(bf16[512,3584]{1,0:T(8,128)(2,1)} %collective-permute-done.3, bf16[128,3584]{1,0:T(8,128)(2,1)S(1)} %broadcast_select_fusion.4, bf16[128,3584]{1,0:T(8,128)(2,1)S(1)} %broadcast_select_fusion.6, bf16[128,3584]{1,0:T(8,128)(2,1)} %broadcast_select_fusion.8, bf16[128,3584]{1,0:T(8,128)(2,1)S(1)} %dynamic-slice_bitcast_fusion.3), kind=kOutput, calls=%fused_computation.98 | convolution fusion | flops 1893728256 | bytes 8388608 | tf_op jit(solution)/shard_map/dot_general | solution.py:93
  302.8 4.3 fusion.35
  307.1 4.6 %fusion.44 = bf16[512,512]{1,0:T(8,128)(2,1)S(1)} fusion(f32[512,512]{1,0:T(8,128)} %collective-permute-done.34, bf16[1,1,512,7168]{3,2,1,0:T(8,128)(2,1)S(1)} %bitcast.79, s32[]{:T(128)S(6)} %select_n.138, f32[512,512]{1,0:T(8,128)} %fusion.35, bf16[128,3584]{1,0:T(8,128)(2,1)} %copy-done.16, bf16[128,3584]{1,0:T(8,128)(2,1)S(1)} %broadcast_select_fusion.6, ...), kind=kOutput, calls=%fused_computation.68 | convolution fusion | flops 1896349696 | bytes 9961476 | tf_op jit(solution)/shard_map/dot_general | solution.py:93
  312.2 8.7 %collective-permute-done.15 = bf16[128,3584]{1,0:T(8,128)(2,1)} collective-permute-done((bf16[128,3584]{1,0:T(8,128)(2,1)}, bf16[128,3584]{1,0:T(8,128)(2,1)}, u32[]{:S(2)}, u32[]{:S(2)}) %collective-permute-start.15) | collective-permute-done | bytes 917536 | tf_op jit(solution)/shard_map/ppermute | solution.py:69
  338.9 17.5 %collective-permute-done.40 = bf16[128,3584]{1,0:T(8,128)(2,1)S(1)} collective-permute-done((bf16[128,3584]{1,0:T(8,128)(2,1)S(1)}, bf16[128,3584]{1,0:T(8,128)(2,1)S(1)}, u32[]{:S(2)}, u32[]{:S(2)}) %collective-permute-start.40) | collective-permute-done | bytes 917536 | tf_op jit(solution)/shard_map/ppermute | solution.py:69
  369.1 10.3 %collective-permute-done.42 = bf16[128,3584]{1,0:T(8,128)(2,1)S(1)} collective-permute-done((bf16[128,3584]{1,0:T(8,128)(2,1)S(1)}, bf16[128,3584]{1,0:T(8,128)(2,1)S(1)}, u32[]{:S(2)}, u32[]{:S(2)}) %collective-permute-start.42) | collective-permute-done | bytes 917536 | tf_op jit(solution)/shard_map/ppermute | solution.py:69
  386.2 4.3 collective-permute-start.43
  390.5 13.0 %select_reduce_fusion = f32[16]{0:T(128)S(1)} fusion(pred[1024,1024]{1,0:T(8,128)(4,1)S(1)} %broadcast_compare_fusion, bf16[128,16,8,128]{3,2,1,0:T(8,128)(2,1)S(1)} %convert_bitcast_fusion, bf16[128,16,8,128]{3,2,1,0:T(8,128)(2,1)S(1)} %convert_bitcast_fusion.1), kind=kOutput, calls=%fused_computation | convolution fusion | flops 4345298944 | bytes 9437248 | tf_op jit(solution)/shard_map/qhd,khd->hqk/dot_general | solution.py:176
  419.5 13.5 %collective-permute-done.45 = bf16[128,3584]{1,0:T(8,128)(2,1)S(1)} collective-permute-done((bf16[128,3584]{1,0:T(8,128)(2,1)S(1)}, bf16[128,3584]{1,0:T(8,128)(2,1)S(1)}, u32[]{:S(2)}, u32[]{:S(2)}) %collective-permute-start.45) | collective-permute-done | bytes 917536 | tf_op jit(solution)/shard_map/ppermute | solution.py:40
  (196 shorter events, 169.5 us)
Async XLA Ops:
  5.0 34.5 %collective-permute-start.2 = (bf16[3584,512]{1,0:T(8,128)(2,1)}, bf16[3584,512]{1,0:T(8,128)(2,1)}, u32[]{:S(2)}, u32[]{:S(2)}) collective-permute-start(bf16[3584,512]{1,0:T(8,128)(2,1)} %dynamic-slice_bitcast_fusion.1), channel_id=1, source_target_pairs={{0,4},{4,0},{1,5},{5,1},{2,6},{6,2},{3,7},{7,3},{8,12},{12,8},{9,1... | collective-permute-start | bytes 11010056 | tf_op jit(solution)/shard_map/ppermute | solution.py:20
  8.4 31.1 %collective-permute-start.3 = (bf16[512,3584]{1,0:T(8,128)(2,1)}, bf16[512,3584]{1,0:T(8,128)(2,1)}, u32[]{:S(2)}, u32[]{:S(2)}) collective-permute-start(bf16[512,3584]{1,0:T(8,128)(2,1)} %dynamic-slice_bitcast_fusion), channel_id=1, source_target_pairs={{0,4},{4,0},{1,5},{5,1},{2,6},{6,2},{3,7},{7,3},{8,12},{12,8},{9,1... | collective-permute-start | bytes 11010056 | tf_op jit(solution)/shard_map/ppermute | solution.py:20
  65.0 50.1 %collective-permute-start.18 = (bf16[128,3584]{1,0:T(8,128)(2,1)S(1)}, bf16[128,3584]{1,0:T(8,128)(2,1)S(1)}, u32[]{:S(2)}, u32[]{:S(2)}) collective-permute-start(bf16[128,3584]{1,0:T(8,128)(2,1)S(1)} %dynamic-slice_bitcast_fusion.2), channel_id=1, source_target_pairs={{0,1},{1,2},{2,3},{4,5},{5,6},{6,7},{8,9},{9,10},{10,11},{12,13},{... | collective-permute-start | bytes 2752520 | tf_op jit(solution)/shard_map/ppermute | solution.py:51
  66.9 48.2 %collective-permute-start.19 = (bf16[128,3584]{1,0:T(8,128)(2,1)S(1)}, bf16[128,3584]{1,0:T(8,128)(2,1)S(1)}, u32[]{:S(2)}, u32[]{:S(2)}) collective-permute-start(bf16[128,3584]{1,0:T(8,128)(2,1)S(1)} %dynamic-slice_bitcast_fusion.2), channel_id=1, source_target_pairs={{1,0},{2,1},{3,2},{5,4},{6,5},{7,6},{9,8},{10,9},{11,10},{13,12},{... | collective-permute-start | bytes 2752520 | tf_op jit(solution)/shard_map/ppermute | solution.py:52
  71.0 33.9 %collective-permute-start.7 = (bf16[128,3712]{1,0:T(8,128)(2,1)}, bf16[128,3712]{1,0:T(8,128)(2,1)S(1)}, u32[]{:S(2)}, u32[]{:S(2)}) collective-permute-start(bf16[128,3712]{1,0:T(8,128)(2,1)} %collective-permute-done.4), channel_id=1, source_target_pairs={{2,3},{6,7},{10,11},{14,15},{18,19},{22,23},{26,27},{30,31}} | collective-permute-start | bytes 2850824 | tf_op jit(solution)/shard_map/ppermute | solution.py:51
  73.7 32.6 %collective-permute-start.6 = (bf16[128,3712]{1,0:T(8,128)(2,1)}, bf16[128,3712]{1,0:T(8,128)(2,1)S(1)}, u32[]{:S(2)}, u32[]{:S(2)}) collective-permute-start(bf16[128,3712]{1,0:T(8,128)(2,1)} %collective-permute-done.5), channel_id=1, source_target_pairs={{1,0},{5,4},{9,8},{13,12},{17,16},{21,20},{25,24},{29,28}} | collective-permute-start | bytes 2850824 | tf_op jit(solution)/shard_map/ppermute | solution.py:52
  112.1 41.1 %collective-permute-start.8 = (f32[512,512]{1,0:T(8,128)S(1)}, f32[512,512]{1,0:T(8,128)S(1)}, u32[]{:S(2)}, u32[]{:S(2)}) collective-permute-start(f32[512,512]{1,0:T(8,128)S(1)} %fusion.58), channel_id=1, source_target_pairs={{0,4},{4,0},{1,5},{5,1},{2,6},{6,2},{3,7},{7,3},{8,12},{12,8},{9,1... | collective-permute-start | bytes 3145736 | tf_op jit(solution)/shard_map/ppermute | solution.py:20
  115.1 26.3 %collective-permute-start.20 = (bf16[128,3584]{1,0:T(8,128)(2,1)S(1)}, bf16[128,3584]{1,0:T(8,128)(2,1)}, u32[]{:S(2)}, u32[]{:S(2)}) collective-permute-start(bf16[128,3584]{1,0:T(8,128)(2,1)S(1)} %collective-permute-done.18), channel_id=1, source_target_pairs={{1,2},{2,3},{5,6},{6,7},{9,10},{10,11},{13,14},{14,15},{17,18},{18... | collective-permute-start | bytes 2752520 | tf_op jit(solution)/shard_map/ppermute | solution.py:51
  117.9 25.3 %collective-permute-start.21 = (bf16[128,3584]{1,0:T(8,128)(2,1)S(1)}, bf16[128,3584]{1,0:T(8,128)(2,1)}, u32[]{:S(2)}, u32[]{:S(2)}) collective-permute-start(bf16[128,3584]{1,0:T(8,128)(2,1)S(1)} %collective-permute-done.19), channel_id=1, source_target_pairs={{1,0},{2,1},{5,4},{6,5},{9,8},{10,9},{13,12},{14,13},{17,16},{18,1... | collective-permute-start | bytes 2752520 | tf_op jit(solution)/shard_map/ppermute | solution.py:52
  149.4 29.1 %collective-permute-start.36 = (bf16[128,3584]{1,0:T(8,128)(2,1)}, bf16[128,3584]{1,0:T(8,128)(2,1)}, u32[]{:S(2)}, u32[]{:S(2)}) collective-permute-start(bf16[128,3584]{1,0:T(8,128)(2,1)} %collective-permute-done.20), channel_id=1, source_target_pairs={{2,3},{6,7},{10,11},{14,15},{18,19},{22,23},{26,27},{30,31}} | collective-permute-start | bytes 2752520 | tf_op jit(solution)/shard_map/ppermute | solution.py:51
  151.6 27.7 %collective-permute-start.35 = (bf16[128,3584]{1,0:T(8,128)(2,1)}, bf16[128,3584]{1,0:T(8,128)(2,1)}, u32[]{:S(2)}, u32[]{:S(2)}) collective-permute-start(bf16[128,3584]{1,0:T(8,128)(2,1)} %collective-permute-done.21), channel_id=1, source_target_pairs={{1,0},{5,4},{9,8},{13,12},{17,16},{21,20},{25,24},{29,28}} | collective-permute-start | bytes 2752520 | tf_op jit(solution)/shard_map/ppermute | solution.py:52
  162.6 29.8 %collective-permute-start.24 = (bf16[256,1280]{1,0:T(8,128)(2,1)S(1)}, bf16[256,1280]{1,0:T(8,128)(2,1)S(1)}, u32[]{:S(2)}, u32[]{:S(2)}) collective-permute-start(bf16[256,1280]{1,0:T(8,128)(2,1)S(1)} %collective-permute-done.22), channel_id=1, source_target_pairs={{1,2},{2,3},{5,6},{6,7},{9,10},{10,11},{13,14},{14,15},{17,18},{18... | collective-permute-start | bytes 1966088 | tf_op jit(solution)/shard_map/ppermute | solution.py:51
  164.5 27.9 %collective-permute-start.25 = (bf16[256,1280]{1,0:T(8,128)(2,1)S(1)}, bf16[256,1280]{1,0:T(8,128)(2,1)S(1)}, u32[]{:S(2)}, u32[]{:S(2)}) collective-permute-start(bf16[256,1280]{1,0:T(8,128)(2,1)S(1)} %collective-permute-done.23), channel_id=1, source_target_pairs={{1,0},{2,1},{5,4},{6,5},{9,8},{10,9},{13,12},{14,13},{17,16},{18,1... | collective-permute-start | bytes 1966088 | tf_op jit(solution)/shard_map/ppermute | solution.py:52
  175.0 67.4 %collective-permute-start.11 = (bf16[128,3584]{1,0:T(8,128)(2,1)S(1)}, bf16[128,3584]{1,0:T(8,128)(2,1)S(1)}, u32[]{:S(2)}, u32[]{:S(2)}) collective-permute-start(bf16[128,3584]{1,0:T(8,128)(2,1)S(1)} %get-tuple-element.40), channel_id=1, source_target_pairs={{3,2},{7,6},{11,10},{15,14},{19,18},{23,22},{27,26},{31,30}} | collective-permute-start | bytes 2752520 | tf_op jit(solution)/shard_map/ppermute | solution.py:69
  178.5 64.0 %collective-permute-start.10 = (bf16[128,3584]{1,0:T(8,128)(2,1)S(1)}, bf16[128,3584]{1,0:T(8,128)(2,1)S(1)}, u32[]{:S(2)}, u32[]{:S(2)}) collective-permute-start(bf16[128,3584]{1,0:T(8,128)(2,1)S(1)} %get-tuple-element.39), channel_id=1, source_target_pairs={{0,1},{4,5},{8,9},{12,13},{16,17},{20,21},{24,25},{28,29}} | collective-permute-start | bytes 2752520 | tf_op jit(solution)/shard_map/ppermute | solution.py:68
  198.2 38.8 %collective-permute-start.26 = (bf16[128,3584]{1,0:T(8,128)(2,1)S(1)}, bf16[128,3584]{1,0:T(8,128)(2,1)S(1)}, u32[]{:S(2)}, u32[]{:S(2)}) collective-permute-start(bf16[128,3584]{1,0:T(8,128)(2,1)S(1)} %dynamic-slice_bitcast_fusion.3), channel_id=1, source_target_pairs={{0,1},{1,2},{2,3},{4,5},{5,6},{6,7},{8,9},{9,10},{10,11},{12,13},{... | collective-permute-start | bytes 2752520 | tf_op jit(solution)/shard_map/ppermute | solution.py:51
  202.3 32.3 %collective-permute-start.29 = (bf16[256,1280]{1,0:T(8,128)(2,1)S(1)}, bf16[256,1280]{1,0:T(8,128)(2,1)S(1)}, u32[]{:S(2)}, u32[]{:S(2)}) collective-permute-start(bf16[256,1280]{1,0:T(8,128)(2,1)S(1)} %collective-permute-done.24), channel_id=1, source_target_pairs={{2,3},{6,7},{10,11},{14,15},{18,19},{22,23},{26,27},{30,31}} | collective-permute-start | bytes 1966088 | tf_op jit(solution)/shard_map/ppermute | solution.py:51
  203.8 33.2 %collective-permute-start.27 = (bf16[128,3584]{1,0:T(8,128)(2,1)S(1)}, bf16[128,3584]{1,0:T(8,128)(2,1)S(1)}, u32[]{:S(2)}, u32[]{:S(2)}) collective-permute-start(bf16[128,3584]{1,0:T(8,128)(2,1)S(1)} %dynamic-slice_bitcast_fusion.3), channel_id=1, source_target_pairs={{1,0},{2,1},{3,2},{5,4},{6,5},{7,6},{9,8},{10,9},{11,10},{13,12},{... | collective-permute-start | bytes 2752520 | tf_op jit(solution)/shard_map/ppermute | solution.py:52
  234.6 68.2 %collective-permute-start.37 = (f32[512,512]{1,0:T(8,128)}, f32[512,512]{1,0:T(8,128)}, u32[]{:S(2)}, u32[]{:S(2)}) collective-permute-start(f32[512,512]{1,0:T(8,128)} %fusion.56), channel_id=1, source_target_pairs={{0,4},{4,0},{1,5},{5,1},{2,6},{6,2},{3,7},{7,3},{8,12},{12,8},{9,1... | collective-permute-start | bytes 3145736 | tf_op jit(solution)/shard_map/ppermute | solution.py:20
  244.2 48.7 %collective-permute-start.13 = (bf16[128,3584]{1,0:T(8,128)(2,1)}, bf16[128,3584]{1,0:T(8,128)(2,1)}, u32[]{:S(2)}, u32[]{:S(2)}) collective-permute-start(bf16[128,3584]{1,0:T(8,128)(2,1)} %get-tuple-element.42), channel_id=1, source_target_pairs={{2,1},{3,2},{6,5},{7,6},{10,9},{11,10},{14,13},{15,14},{18,17},{19... | collective-permute-start | bytes 2752520 | tf_op jit(solution)/shard_map/ppermute | solution.py:69
  246.1 46.8 %collective-permute-start.12 = (bf16[128,3584]{1,0:T(8,128)(2,1)}, bf16[128,3584]{1,0:T(8,128)(2,1)}, u32[]{:S(2)}, u32[]{:S(2)}) collective-permute-start(bf16[128,3584]{1,0:T(8,128)(2,1)} %get-tuple-element.41), channel_id=1, source_target_pairs={{0,1},{1,2},{4,5},{5,6},{8,9},{9,10},{12,13},{13,14},{16,17},{17,1... | collective-permute-start | bytes 2752520 | tf_op jit(solution)/shard_map/ppermute | solution.py:68
  299.2 24.9 %collective-permute-start.14 = (bf16[128,3584]{1,0:T(8,128)(2,1)}, bf16[128,3584]{1,0:T(8,128)(2,1)}, u32[]{:S(2)}, u32[]{:S(2)}) collective-permute-start(bf16[128,3584]{1,0:T(8,128)(2,1)} %get-tuple-element.43), channel_id=1, source_target_pairs={{0,1},{1,2},{2,3},{4,5},{5,6},{6,7},{8,9},{9,10},{10,11},{12,13},{... | collective-permute-start | bytes 2752520 | tf_op jit(solution)/shard_map/ppermute | solution.py:68
  365.9 42.2 %collective-permute-start.16 = (bf16[128,3584]{1,0:T(8,128)(2,1)S(1)}, bf16[128,3584]{1,0:T(8,128)(2,1)}, u32[]{:S(2)}, u32[]{:S(2)}) collective-permute-start(bf16[128,3584]{1,0:T(8,128)(2,1)S(1)} %fusion.26), channel_id=1, source_target_pairs={{0,8},{8,16},{16,24},{1,9},{9,17},{17,25},{2,10},{10,18},{18,26},{... | collective-permute-start | bytes 2752520 | tf_op jit(solution)/shard_map/ppermute | solution.py:40
  408.1 28.7 %collective-permute-start.17 = (bf16[128,3584]{1,0:T(8,128)(2,1)}, bf16[128,3584]{1,0:T(8,128)(2,1)S(1)}, u32[]{:S(2)}, u32[]{:S(2)}) collective-permute-start(bf16[128,3584]{1,0:T(8,128)(2,1)} %collective-permute-done.16), channel_id=1, source_target_pairs={{0,4},{4,0},{1,5},{5,1},{2,6},{6,2},{3,7},{7,3},{8,12},{12,8},{9,1... | collective-permute-start | bytes 2752520 | tf_op jit(solution)/shard_map/ppermute | solution.py:20
  (53 other events, 1108.9 us)
